TPU v7x, 32 devices: a whole 2x2x4 slice. The times are simulated.
32 devices in a mesh: gx: 4 (over y, x), gy: 8 (over z, core).
Axes of the slice: x: 2, y: 2, z: 4, core: 2. Of those that a mesh axis runs over, the one named last changes fastest.
Arguments:
- fields: float32 [8, 12, 64, 128], P(None, 'gx', 'gy'), may hold values from -2.1 to 2.1, as said below
- shear_offset: int32 [1], replicated, may hold values from 0 to 63
- row_shift: int32 [12], P('gx'), may hold values from 0 to 63
Outputs:
- advanced: float32 [8, 12, 64, 128], P(None, 'gx', 'gy')
Inputs may be any that keep to these rules, and one draw needn't show every extreme that they name: `fields`: component 0 is a density of at least 0.5 and at most 2; component 4 lies between 0 and component 0.
All inputs are finite; a program needn't handle non-finite values.
Results may differ from a plain program's by a relative error of at most 0.00002.
Values sent between devices are 32-bit elements; how exact they have to be, the bound alone decides.
No kernel may reach another device: no remote copies, remote signals or barrier semaphores. Data moves between devices by JAX's collectives and lax.ppermute only.
A program may use at most 64 MiB of HBM per device.

v0:
```python
import jax
import jax.numpy as jnp
from jax import lax
from jax.sharding import PartitionSpec as P

time_step = 0.2
sound_squared = 1.0
shear_speed = 1.5
sweep_orders = ((0, 1, 2), (1, 2, 0), (2, 0, 1))


def with_halo(block, sides, width):
    for axis, dim in sides:
        count = lax.axis_size(axis)
        forward = [(i, i + 1) for i in range(count - 1)]
        forward.append((count - 1, 0))
        backward = [(target, source) for source, target in forward]
        low = lax.ppermute(
            lax.slice_in_dim(block, block.shape[dim] - width, None, axis=dim), axis, forward
        )
        high = lax.ppermute(lax.slice_in_dim(block, 0, width, axis=dim), axis, backward)
        block = jnp.concatenate([low, block, high], axis=dim)
    return block


def from_behind(shard, axis, by):
    count = lax.axis_size(axis)
    return lax.ppermute(shard, axis, [(i, (i + by) % count) for i in range(count)])


def minmod(first_diff, second_diff):
    return jnp.maximum(0.0, jnp.minimum(first_diff, second_diff)) + jnp.minimum(
        0.0, jnp.maximum(first_diff, second_diff)
    )


def edge_states(values, direction):
    if direction == 2:
        lower_cell = jnp.roll(values, 1, axis=2)
        upper_cell = jnp.roll(values, -1, axis=2)
        gradient = minmod(values - lower_cell, upper_cell - values)
        left_face = jnp.roll(values + 0.5 * gradient, 1, axis=2)
        right_face = values - 0.5 * gradient
        return (left_face, right_face)
    extent = values.shape[direction]
    lower_cell = lax.slice_in_dim(values, 0, extent - 2, axis=direction)
    middle = lax.slice_in_dim(values, 1, extent - 1, axis=direction)
    upper_cell = lax.slice_in_dim(values, 2, extent, axis=direction)
    gradient = minmod(middle - lower_cell, upper_cell - middle)
    left_face = lax.slice_in_dim(middle + 0.5 * gradient, 0, extent - 3, axis=direction)
    right_face = lax.slice_in_dim(middle - 0.5 * gradient, 1, extent - 2, axis=direction)
    return (left_face, right_face)


def side_terms(primitive, normal_field):
    density, normal_vel, tang_one, tang_two, field_one, field_two, fraction = primitive
    pressure = sound_squared * density + 0.5 * (
        normal_field * normal_field + field_one * field_one + field_two * field_two
    )
    fluxes = (
        density * normal_vel,
        density * normal_vel * normal_vel + pressure - normal_field * normal_field,
        density * normal_vel * tang_one - normal_field * field_one,
        density * normal_vel * tang_two - normal_field * field_two,
        normal_vel * field_one - tang_one * normal_field,
        normal_vel * field_two - tang_two * normal_field,
        density * fraction * normal_vel,
    )
    conserved = (
        density,
        density * normal_vel,
        density * tang_one,
        density * tang_two,
        field_one,
        field_two,
        density * fraction,
    )
    normal_alfven = normal_field * normal_field / density
    tangent_alfven = (field_one * field_one + field_two * field_two) / density
    spread = (
        (sound_squared - normal_alfven) ** 2
        + tangent_alfven * tangent_alfven
        + 2.0 * tangent_alfven * (sound_squared + normal_alfven)
    )
    fast_speed = jnp.sqrt(0.5 * (sound_squared + normal_alfven + tangent_alfven + jnp.sqrt(spread)))
    return (fluxes, conserved, normal_vel - fast_speed, normal_vel + fast_speed)


def hll_flux(left_side, right_side, normal_field):
    flux_left_all, cons_left_all, low_left, high_left = side_terms(left_side, normal_field)
    flux_right_all, cons_right_all, low_right, high_right = side_terms(right_side, normal_field)
    lower_speed = jnp.minimum(jnp.minimum(low_left, low_right), 0.0)
    upper_speed = jnp.maximum(jnp.maximum(high_left, high_right), 0.0)
    inverse_gap = 1.0 / (upper_speed - lower_speed)
    return tuple(
        (
            (
                upper_speed * flux_left
                - lower_speed * flux_right
                + lower_speed * upper_speed * (cons_right - cons_left)
            )
            * inverse_gap
            for flux_left, flux_right, cons_left, cons_right in zip(
                flux_left_all, flux_right_all, cons_left_all, cons_right_all
            )
        )
    )


def sweep(density, velocity, fraction, centres, faces, direction, window):
    normal_axis, first_axis, second_axis = sweep_orders[direction]
    states = (
        density,
        velocity[normal_axis],
        velocity[first_axis],
        velocity[second_axis],
        centres[first_axis],
        centres[second_axis],
        fraction,
    )
    states = tuple((window(values) for values in states))
    face_pairs = [edge_states(values, direction) for values in states]
    left_side = tuple((pair_item[0] for pair_item in face_pairs))
    right_side = tuple((pair_item[1] for pair_item in face_pairs))
    normal_face = window(faces[direction])
    if direction == 2:
        normal_field = normal_face
    else:
        extent = normal_face.shape[direction]
        normal_field = lax.slice_in_dim(normal_face, 2, extent - 1, axis=direction)
    return hll_flux(left_side, right_side, normal_field)


def momentum_parts(fluxes, direction):
    normal_axis, first_axis, second_axis = sweep_orders[direction]
    parts = [fluxes[1], fluxes[1], fluxes[1]]
    parts[normal_axis] = fluxes[1]
    parts[first_axis] = fluxes[2]
    parts[second_axis] = fluxes[3]
    return parts


def predict(padded):
    cells_x = padded.shape[1] - 6
    cells_y = padded.shape[2] - 6
    face_x, face_y, face_z = (padded[5], padded[6], padded[7])
    centres = (
        (0.5 * (face_x[:-1] + face_x[1:]))[:, :-1],
        (0.5 * (face_y[:, :-1] + face_y[:, 1:]))[:-1],
        (0.5 * (face_z + jnp.roll(face_z, -1, axis=2)))[:-1, :-1],
    )
    density = padded[0][:-1, :-1]
    inverse = 1.0 / density
    velocity = tuple((padded[component][:-1, :-1] * inverse for component in (1, 2, 3)))
    fraction = padded[4][:-1, :-1] * inverse
    faces = (face_x[:-1, :-1], face_y[:-1, :-1], face_z[:-1, :-1])
    flux_x = sweep(
        density, velocity, fraction, centres, faces, 0, lambda values: values[:, 2 : cells_y + 4]
    )
    flux_y = sweep(
        density, velocity, fraction, centres, faces, 1, lambda values: values[2 : cells_x + 4]
    )
    flux_z = sweep(
        density,
        velocity,
        fraction,
        centres,
        faces,
        2,
        lambda values: values[2 : cells_x + 4, 2 : cells_y + 4],
    )

    def diverge(along_x, along_y, along_z):
        return (
            along_x[2 : cells_x + 2, 1 : cells_y + 1]
            - along_x[1 : cells_x + 1, 1 : cells_y + 1]
            + along_y[1 : cells_x + 1, 2 : cells_y + 2]
            - along_y[1 : cells_x + 1, 1 : cells_y + 1]
            + (jnp.roll(along_z, -1, axis=2) - along_z)[1 : cells_x + 1, 1 : cells_y + 1]
        )

    def own_cells(component):
        return padded[component][3 : cells_x + 3, 3 : cells_y + 3]

    parts_x = momentum_parts(flux_x, 0)
    parts_y = momentum_parts(flux_y, 1)
    parts_z = momentum_parts(flux_z, 2)
    new_density = own_cells(0) - time_step * diverge(flux_x[0], flux_y[0], flux_z[0])
    new_momentum = [
        own_cells(1 + component)
        - time_step * diverge(parts_x[component], parts_y[component], parts_z[component])
        for component in range(3)
    ]
    new_dye = own_cells(4) - time_step * diverge(flux_x[6], flux_y[6], flux_z[6])
    edge_z = 0.25 * (
        -flux_x[4][1 : cells_x + 2, 1 : cells_y + 2]
        - flux_x[4][1 : cells_x + 2, 0 : cells_y + 1]
        + flux_y[5][1 : cells_x + 2, 1 : cells_y + 2]
        + flux_y[5][0 : cells_x + 1, 1 : cells_y + 2]
    )
    across_x = flux_x[5][1 : cells_x + 2, 1 : cells_y + 1]
    edge_y = 0.25 * (
        across_x
        + jnp.roll(across_x, 1, axis=2)
        - flux_z[4][1 : cells_x + 2, 1 : cells_y + 1]
        - flux_z[4][0 : cells_x + 1, 1 : cells_y + 1]
    )
    across_y = flux_y[4][1 : cells_x + 1, 1 : cells_y + 2]
    edge_x = 0.25 * (
        -across_y
        - jnp.roll(across_y, 1, axis=2)
        + flux_z[5][1 : cells_x + 1, 1 : cells_y + 2]
        + flux_z[5][1 : cells_x + 1, 0 : cells_y + 1]
    )
    low_y = edge_y[0:cells_x]
    new_bx = (
        own_cells(5)
        - time_step * (edge_z[0:cells_x, 1 : cells_y + 1] - edge_z[0:cells_x, 0:cells_y])
        + time_step * (jnp.roll(low_y, -1, axis=2) - low_y)
    )
    low_x = edge_x[:, 0:cells_y]
    new_by = (
        own_cells(6)
        - time_step * (jnp.roll(low_x, -1, axis=2) - low_x)
        + time_step * (edge_z[1 : cells_x + 1, 0:cells_y] - edge_z[0:cells_x, 0:cells_y])
    )
    new_bz = (
        own_cells(7)
        - time_step * (edge_y[1 : cells_x + 1] - edge_y[0:cells_x])
        + time_step * (edge_x[:, 1 : cells_y + 1] - edge_x[:, 0:cells_y])
    )
    return jnp.stack([new_density] + new_momentum + [new_dye, new_bx, new_by, new_bz])


def roll_loop(blocks, quotient, leftover, cycle_size, block_rows, advance, previous):
    carried = blocks
    for section_bit in range(cycle_size.bit_length() - 1):
        arrived = advance(carried, 1 << section_bit)
        carried = jnp.where(quotient // (1 << section_bit) % 2 == 1, arrived, carried)
    before = previous(carried)
    row_axis = blocks.ndim - 2
    united = jnp.concatenate([before, carried], axis=row_axis)
    length = blocks.shape[row_axis]
    positions = block_rows - leftover + jnp.arange(length, dtype=jnp.int32).reshape(length, 1)
    positions = jnp.broadcast_to(positions, blocks.shape)
    return jnp.take_along_axis(united, positions, axis=row_axis)


def on_device(fields, shear_offset, row_shift):
    cells_x = fields.shape[1]
    cells_y = fields.shape[2]
    count_y = lax.axis_size("gy")
    count_x = lax.axis_size("gx")
    offset = shear_offset[0]
    quotient = offset // cells_y
    remainder = offset % cells_y
    padded = with_halo(fields, (("gx", 1),), 3)
    strips = jnp.stack([padded[:, :3], padded[:, cells_x + 3 :]])
    strip_quot = jnp.stack([count_y - 1 - quotient, quotient]).reshape(2, 1, 1, 1, 1)
    strip_rest = jnp.stack([cells_y - remainder, remainder]).reshape(2, 1, 1, 1, 1)
    rolled = roll_loop(
        strips,
        strip_quot,
        strip_rest,
        count_y,
        cells_y,
        lambda operand, distance: from_behind(operand, "gy", distance),
        lambda operand: from_behind(operand, "gy", 1),
    )
    signs = jnp.array([1.0, -1.0], jnp.float32).reshape(2, 1, 1, 1)
    shear_momentum = rolled[:, 2] + shear_speed * signs * rolled[:, 0]
    rolled = jnp.concatenate([rolled[:, :2], shear_momentum[:, None], rolled[:, 3:]], axis=1)
    place_x = lax.axis_index("gx")
    low_rim = jnp.where(place_x == 0, rolled[0], padded[:, :3])
    high_rim = jnp.where(place_x == count_x - 1, rolled[1], padded[:, cells_x + 3 :])
    padded = jnp.concatenate([low_rim, padded[:, 3 : cells_x + 3], high_rim], axis=1)
    padded = with_halo(padded, (("gy", 2),), 3)
    updated = predict(padded)
    row_quot = (row_shift // cells_y).reshape(1, cells_x, 1, 1)
    row_rest = (row_shift % cells_y).reshape(1, cells_x, 1, 1)
    result = roll_loop(
        updated,
        row_quot,
        row_rest,
        count_y,
        cells_y,
        lambda operand, distance: from_behind(operand, "gy", distance),
        lambda operand: from_behind(operand, "gy", 1),
    )
    return result


def solution(mesh):
    placed = (P(None, "gx", "gy", None), P(), P("gx"))
    return jax.shard_map(
        on_device, mesh=mesh, in_specs=placed, out_specs=P(None, "gx", "gy", None), check_vma=False
    )
```

profile of v0, /device:TPU:0, one launch (start us, length us, event | category | flops | bytes accessed | tf_op | source)
XLA Modules:
  0.0 870.4 jit_solution(16667696247054854610)
XLA Ops:
  0.0 2.9 collective-permute-start
  2.9 1.0 collective-permute-start.1
  4.8 2.8 collective-permute-done
  7.6 1.7 collective-permute-done.1
  9.4 6.9 collective-permute-done.2
  16.5 7.9 collective-permute-done.3
  24.6 7.7 collective-permute-done.4
  32.5 6.8 collective-permute-done.5
  39.3 556.3 %gather_fusion = f32[49152]{0:T(1024)S(1)} fusion(f32[2,8,3,16,128]{4,3,2,1,0:T(8,128)S(1)} %pad_maximum_fusion.1, s32[49152]{0:T(1024)S(1)} %bitcast.88), kind=kCustom, calls=%fused_computation | custom fusion | bytes 1376256 | tf_op jit(solution)/shard_map/jit(take_along_axis)/gather | solution.py:246
  595.8 0.5 copy-done.1
  596.4 0.8 copy-done
  597.3 3.5 collective-permute-start.7
  600.9 2.8 collective-permute-done.6
  605.2 0.2 multiply_sqrt_fusion
  605.4 0.1 multiply_sqrt_fusion.3
  606.7 0.1 multiply_sqrt_fusion.1
  606.9 0.2 add_multiply_fusion.7
  607.3 0.2 add_multiply_fusion.10
  609.9 5.8 collective-permute-done.8
  615.9 7.4 collective-permute-done.9
  623.5 5.4 collective-permute-done.10
  629.1 5.7 collective-permute-done.11
  634.8 234.9 %gather_fusion.1 = f32[24576]{0:T(1024)S(1)} fusion(f32[8,3,16,128]{3,2,1,0:T(8,128)S(1)} %pad_maximum_fusion.5, s32[24576]{0:T(1024)S(1)} %bitcast.89), kind=kCustom, calls=%fused_computation.1 | custom fusion | bytes 589824 | tf_op jit(solution)/shard_map/jit(take_along_axis)/gather | solution.py:246
  869.7 0.7 fusion.5
  (118 shorter events, 7.1 us)
Async XLA Ops:
  0.0 7.6 collective-permute-start
  2.9 6.3 collective-permute-start.1
  9.3 6.9 collective-permute-start.2
  16.3 8.0 collective-permute-start.3
  24.4 8.0 copy-start.2
  24.4 7.8 collective-permute-start.4
  32.3 6.9 collective-permute-start.5
  595.7 0.7 copy-start.1
  596.3 0.9 copy-start
  597.3 6.4 collective-permute-start.6
  597.3 6.4 collective-permute-start.7
  609.8 5.9 collective-permute-start.8
  615.8 7.5 collective-permute-start.9
  623.3 5.5 collective-permute-start.10
  629.0 5.8 collective-permute-start.11
where the time goes:
time: 871 us; the launch traced here: 870 us
  local copies, waits for them, and re-layouts  795 us (91%)
  waiting for transfers between devices  60.8 us (7%)
    gather x2, local copies, waits for them, and re-layouts, roll_loop(): return jnp.take_along_axis(united, positions, axis=row_axis)  791 us
    ppermute x8, waiting for transfers between devices, from_behind(): lax.ppermute(shard, axis, [(i, (i + by) % count) for i in range(count)])  53.6 us
  transfers between devices with their start and end apart: 12, of which 11 were waited for; matrix products, arithmetic and copies ran while one was open for 0% of the time, Pallas kernels for 0%

commit v1 on v0

v1 whole, which is shorter than its diff:
```python
import functools
import jax
import jax.numpy as jnp
from jax import lax
from jax.experimental import pallas as pl
from jax.experimental.pallas import tpu as pltpu
from jax.sharding import PartitionSpec as P

time_step = 0.2
sound_squared = 1.0
shear_speed = 1.5
sweep_orders = ((0, 1, 2), (1, 2, 0), (2, 0, 1))


def remainder(value, by):
    return value & (by - 1) if by & (by - 1) == 0 else lax.rem(value, by)


def quotient(value, by):
    return value >> (by.bit_length() - 1) if by & (by - 1) == 0 else lax.div(value, by)


def minmod(first_diff, second_diff):
    return jnp.maximum(0.0, jnp.minimum(first_diff, second_diff)) + jnp.minimum(
        0.0, jnp.maximum(first_diff, second_diff)
    )


def shift(values, by, axis):
    return pltpu.roll(values, by % values.shape[axis], axis=axis)


def side_terms(state, normal_field):
    density, normal_vel, tang_one, tang_two, field_one, field_two, fraction = state
    normal_square = normal_field * normal_field
    tangent_square = field_one * field_one + field_two * field_two
    mass_flux = density * normal_vel
    dye = density * fraction
    fluxes = (
        mass_flux,
        mass_flux * normal_vel + sound_squared * density + 0.5 * (tangent_square - normal_square),
        mass_flux * tang_one - normal_field * field_one,
        mass_flux * tang_two - normal_field * field_two,
        normal_vel * field_one - tang_one * normal_field,
        normal_vel * field_two - tang_two * normal_field,
        dye * normal_vel,
    )
    conserved = (
        density,
        mass_flux,
        density * tang_one,
        density * tang_two,
        field_one,
        field_two,
        dye,
    )
    inverse = 1.0 / density
    normal_alfven = normal_square * inverse
    tangent_alfven = tangent_square * inverse
    apart = sound_squared - normal_alfven
    spread = (
        apart * apart
        + tangent_alfven * tangent_alfven
        + 2.0 * tangent_alfven * (sound_squared + normal_alfven)
    )
    fast_speed = jnp.sqrt(0.5 * (sound_squared + normal_alfven + tangent_alfven + jnp.sqrt(spread)))
    return (fluxes, conserved, normal_vel - fast_speed, normal_vel + fast_speed)


def hll_flux(left_side, right_side, normal_field):
    flux_left_all, cons_left_all, low_left, high_left = side_terms(left_side, normal_field)
    flux_right_all, cons_right_all, low_right, high_right = side_terms(right_side, normal_field)
    lower_speed = jnp.minimum(jnp.minimum(low_left, low_right), 0.0)
    upper_speed = jnp.maximum(jnp.maximum(high_left, high_right), 0.0)
    inverse_gap = 1.0 / (upper_speed - lower_speed)
    upper = upper_speed * inverse_gap
    lower = lower_speed * inverse_gap
    product = lower_speed * upper
    return tuple(
        upper * flux_left - lower * flux_right + product * (cons_right - cons_left)
        for flux_left, flux_right, cons_left, cons_right in zip(
            flux_left_all, flux_right_all, cons_left_all, cons_right_all
        )
    )


def low_windows(cells_x):
    return [(i, i + k) for i in range(cells_x) for k in (-2, -1) if i + k < 0]


def high_windows(cells_x):
    return [(i, i + k) for i in range(cells_x) for k in (1, 2) if i + k >= cells_x]


def tile_reader(source, start, length, first_tile, tiles):
    cells_y, cells_z = source.shape[3:]
    blocks = length // cells_y
    block = quotient(start, cells_y)
    turn = remainder(start, cells_y)
    inside = lax.broadcasted_iota(jnp.int32, (cells_y, cells_z), 0) < cells_y - turn
    places = [remainder(block + first_tile + k + blocks, blocks) for k in range(tiles + 1)]

    def read(component, row):
        turned = [pltpu.roll(source[place, component, row], cells_y - turn, axis=0) for place in places]
        return [jnp.where(inside, turned[k], turned[k + 1]) for k in range(tiles)]

    return read


class Row:
    def __init__(self, known):
        self.known = dict(known)

    def get(self, *key):
        if key not in self.known:
            getattr(self, "make_" + key[0])(*key[1:-1])
        return self.known[key]

    def all(self, *key):
        return tuple(self.get(*key, item) for item in range(7))

    def put(self, key, values):
        for item, value in enumerate(values):
            self.known[key + (item,)] = value

    def make_cell(self, k):
        raw = [self.get("raw", k, component) for component in range(8)]
        inverse = 1.0 / raw[0]
        self.put(
            ("cell", k),
            (
                raw[0],
                raw[1] * inverse,
                raw[2] * inverse,
                raw[3] * inverse,
                0.5 * (raw[6] + shift(raw[6], -1, 0)),
                0.5 * (raw[7] + shift(raw[7], -1, 1)),
                raw[4] * inverse,
            ),
        )

    def make_centre_x(self, k):
        self.put(("centre_x", k), [0.5 * (self.get("raw", k, 5) + self.get("raw", k + 1, 5))])

    def make_slope(self, k):
        three = [self.all("cell", k + step) for step in (-1, 0, 1)]
        self.put(("slope", k), [0.5 * minmod(h - b, a - h) for b, h, a in zip(*three)])

    def make_along_0(self, face):
        left = [w + s for w, s in zip(self.all("cell", face + 1), self.all("slope", face + 1))]
        right = [w - s for w, s in zip(self.all("cell", face + 2), self.all("slope", face + 2))]
        self.put(("along_0", face), hll_flux(left, right, self.get("raw", face + 2, 5)))

    def sweep(self, k, direction, axis):
        density, vel_x, vel_y, vel_z, centre_y, centre_z, fraction = self.all("cell", k)
        velocity = (vel_x, vel_y, vel_z)
        centres = (self.get("centre_x", k, 0), centre_y, centre_z)
        normal_axis, first_axis, second_axis = sweep_orders[direction]
        states = (
            density,
            velocity[normal_axis],
            velocity[first_axis],
            velocity[second_axis],
            centres[first_axis],
            centres[second_axis],
            fraction,
        )
        left, right = [], []
        for w in states:
            half = 0.5 * minmod(w - shift(w, 1, axis), shift(w, -1, axis) - w)
            left.append(shift(w + half, 1, axis))
            right.append(w - half)
        return hll_flux(left, right, self.get("raw", k, 5 + direction))

    def make_along_1(self, k):
        self.put(("along_1", k), self.sweep(k, 1, 0))

    def make_along_2(self, k):
        self.put(("along_2", k), self.sweep(k, 2, 1))

    def make_out(self):
        along_x = [self.all("along_0", face) for face in range(2)]
        along_y, along_z = self.all("along_1", 2), self.all("along_2", 2)
        edge_z = [
            0.25
            * (
                self.get("along_1", face + 2, 5)
                + self.get("along_1", face + 1, 5)
                - along_x[face][4]
                - shift(along_x[face][4], 1, 0)
            )
            for face in range(2)
        ]
        edge_y = [
            0.25
            * (
                along_x[face][5]
                + shift(along_x[face][5], 1, 1)
                - self.get("along_2", face + 2, 4)
                - self.get("along_2", face + 1, 4)
            )
            for face in range(2)
        ]
        edge_x = 0.25 * (
            along_z[5] + shift(along_z[5], 1, 0) - along_y[4] - shift(along_y[4], 1, 1)
        )
        own = [self.get("raw", 2, component) for component in range(8)]
        places = ((1, 2, 3), (3, 1, 2), (2, 3, 1))
        values = []
        for component in range(5):
            if component == 0:
                slots = (0, 0, 0)
            elif component == 4:
                slots = (6, 6, 6)
            else:
                slots = tuple(places[d][component - 1] for d in range(3))
            through_y, through_z = along_y[slots[1]], along_z[slots[2]]
            total = (
                along_x[1][slots[0]]
                - along_x[0][slots[0]]
                + shift(through_y, -1, 0)
                - through_y
                + shift(through_z, -1, 1)
                - through_z
            )
            values.append(own[component] - time_step * total)
        values.append(
            own[5]
            - time_step * (shift(edge_z[0], -1, 0) - edge_z[0])
            + time_step * (shift(edge_y[0], -1, 1) - edge_y[0])
        )
        values.append(
            own[6]
            - time_step * (shift(edge_x, -1, 1) - edge_x)
            + time_step * (edge_z[1] - edge_z[0])
        )
        values.append(
            own[7]
            - time_step * (edge_y[1] - edge_y[0])
            + time_step * (shift(edge_x, -1, 0) - edge_x)
        )
        self.put(("out",), values)


def message(wanted):
    mains, slots = [], []
    for row, radial in wanted:
        k = radial - row + 2
        if k in (1, 3):
            mains += [(row, "raw", k, component) for component in range(8)]
            slots += [[(row, "raw", k, component)] for component in (0, 1, 2, 5, 6, 7)]
        else:
            mains += [(row, "cell", k, item) for item in range(7)]
            slots += [[(row, "cell", k, item) for item in pair] for pair in ((0, 1), (2, 4), (5,))]
            if k == 4:
                mains.append((row, "raw", k, 5))
                slots.append([(row, "raw", k, 5)])
    return mains, slots


def message_tiles(wanted):
    mains, slots = message(wanted)
    return len(mains) + (len(slots) + 1) // 2


def pack(out, wanted, values):
    mains, slots = message(wanted)
    sub = lax.broadcasted_iota(jnp.int32, out.shape[1:], 0)
    rows = out.shape[1]
    for at, (row, *key) in enumerate(mains):
        out[at] = values[row].get(*key)[:rows]

    def slot(keys):
        around = [values[row].get(*key)[rows:] for row, *key in keys]
        first = around[0]
        tile = jnp.where(sub < 2, first, shift(first, 4, 0))
        if len(around) == 2:
            second = around[1]
            tile = jnp.where(sub == 1, shift(second, 1, 0), tile)
            tile = jnp.where(sub == 2, shift(second, 3, 0), tile)
        return tile

    for at in range(0, len(slots), 2):
        tile = slot(slots[at])
        if at + 1 < len(slots):
            tile = jnp.where(sub < 4, tile, shift(slot(slots[at + 1]), 4, 0))
        out[len(mains) + at // 2] = tile


def unpack(source, wanted, known):
    mains, slots = message(wanted)
    sub = lax.broadcasted_iota(jnp.int32, source.shape[1:], 0)
    edges = {}
    for at, keys in enumerate(slots):
        tile = source[len(mains) + at // 2]
        turned = shift(tile, 4, 0)
        one, two = (tile, turned) if at % 2 == 0 else (turned, tile)
        around = jnp.where(sub < 4, one, two)
        edges[keys[0]] = around
        if len(keys) == 2:
            edges[keys[1]] = jnp.where(sub < 4, shift(around, -1, 0), shift(around, 1, 0))
    for at, key in enumerate(mains):
        main = source[at]
        known[key[0]][key[1:]] = jnp.concatenate([main, edges.get(key, main)], axis=0)


def windows_call(near, far, received, swapped, offset):
    count = len(near)
    parts, cells_x, cells_y, cells_z = near[0].shape
    blocks = 2 * count
    length = blocks * cells_y
    lows, highs = low_windows(cells_x), high_windows(cells_x)

    def body(offset, received, swapped, *refs):
        ins, whole, outs = refs[:blocks], refs[blocks], refs[blocks + 1 : -2]
        shifts, sems = refs[-2:]
        copies = [
            pltpu.make_async_copy(source, shifts.at[at], sems.at[at])
            for at, source in enumerate((received, swapped))
        ]
        for copy in copies:
            copy.start()
        place_x, place_y = lax.axis_index("gx"), lax.axis_index("gy")
        last = lax.axis_size("gx") - 1
        for side in range(2):
            for step in range(count):
                block = ins[side * count + step]
                place = remainder((place_y ^ side) - 2 * step + blocks, blocks)
                if side == 0 and step == 0:
                    whole[place, : parts // 2] = block[parts // 2 :]
                    whole[place, parts // 2 :] = block[: parts // 2]
                else:
                    whole[place] = block[...]
        sub = lax.broadcasted_iota(jnp.int32, (cells_y, cells_z), 0)
        for copy in copies:
            copy.wait()
        here = remainder(place_x + place_y, 2) == 0
        above, below = (
            [jnp.where(here, shifts[one, i], shifts[1 - one, i]) for i in range(cells_x)]
            for one in range(2)
        )
        for out, shift_by, wanted, end, sign, turn in (
            (outs[0], above, lows, last, 1, cells_x),
            (outs[1], below, highs, 0, -1, -cells_x),
        ):
            at_end = place_x == end
            away = jnp.where(at_end, sign * offset[0], 0)
            boost = jnp.where(at_end, sign * shear_speed, 0.0)
            known = {}
            for row, radial in wanted:
                start = remainder(place_y * cells_y - shift_by[row] + away + 2 * length, length)
                read = tile_reader(whole, start, length, -1, 3)
                raw = []
                for component in range(parts):
                    before, main, after = read(component, radial + turn)
                    raw.append(jnp.concatenate([main, jnp.where(sub < 4, after, before)], axis=0))
                raw[2] = raw[2] + boost * raw[0]
                for component in range(parts):
                    known.setdefault(row, {})["raw", radial - row + 2, component] = raw[component]
            pack(out, wanted, {row: Row(found) for row, found in known.items()})

    vmem = pl.BlockSpec(memory_space=pltpu.VMEM)
    smem = pl.BlockSpec(memory_space=pltpu.SMEM)
    return pl.pallas_call(
        body,
        out_shape=[jax.ShapeDtypeStruct((blocks, parts, cells_x, cells_y, cells_z), jnp.float32)]
        + [
            jax.ShapeDtypeStruct((message_tiles(wanted), cells_y, cells_z), jnp.float32)
            for wanted in (lows, highs)
        ],
        in_specs=[smem] + [vmem] * (2 + blocks),
        out_specs=[vmem] * 3,
        scratch_shapes=[pltpu.SMEM((2, cells_x), jnp.int32), pltpu.SemaphoreType.DMA((2,))],
        compiler_params=pltpu.CompilerParams(vmem_limit_bytes=32 * 1024 * 1024),
        name="windows",
    )(offset, received, swapped, *near, *far)


def reads(key):
    name, *rest = key
    if name == "out":
        found = [("raw", 2, component) for component in range(8)]
        found += [("along_0", face, item) for face in range(2) for item in range(7)]
        found += [(along, 2, item) for along in ("along_1", "along_2") for item in range(7)]
        return found + [(along, k, item) for k in (1, 3) for along, item in (("along_1", 5), ("along_2", 4))]
    if name == "cell":
        return [("raw", rest[0], component) for component in range(8)]
    if name == "centre_x":
        return [("raw", rest[0], 5), ("raw", rest[0] + 1, 5)]
    if name == "slope":
        return [("cell", rest[0] + step, rest[1]) for step in (-1, 0, 1)]
    if name == "along_0":
        cells = [rest[0] + 1, rest[0] + 2]
        found = [(of, k, item) for k in cells for of in ("cell", "slope") for item in range(7)]
        return found + [("raw", cells[1], 5)]
    found = [("cell", rest[0], item) for item in range(7)] + [("centre_x", rest[0], 0)]
    return found + [("raw", rest[0], {"along_1": 6, "along_2": 7}[name])]


def handed_on(cells_x):
    plans = []
    for row in range(cells_x):

        def stage_of_ghost(k):
            return 0 if 0 <= row + k - 2 < cells_x else 1 if row + k - 2 >= cells_x else 2

        stages, readers = {}, {}

        def stage(key):
            if key not in stages:
                given = key[0] == "raw" or (key[0] == "cell" and key[1] in (0, 4) and stage_of_ghost(key[1]))
                if given:
                    stages[key] = stage_of_ghost(key[1])
                else:
                    stages[key] = max(stage(found) for found in reads(key))
                    for found in reads(key):
                        readers.setdefault(found, []).append(key)
            return stages[key]

        ends = [("out", component) for component in range(8)]
        for key in ends:
            stage(key)
        plans.append(
            [
                [
                    key
                    for key, at in stages.items()
                    if at == level
                    and (key in ends or any(stages[reader] > level for reader in readers[key]))
                ]
                for level in range(2)
            ]
        )
    return plans


def own_windows(wholes, row, row_shift, known):
    _, parts, cells_x, cells_y, cells_z = wholes.shape
    length = wholes.shape[0] * cells_y
    sub = lax.broadcasted_iota(jnp.int32, (cells_y, cells_z), 0)
    start = remainder(lax.axis_index("gy") * cells_y - row_shift[row] + length, length)
    read = tile_reader(wholes, start, length, -1, 3)
    for k in range(5):
        radial = row + k - 2
        if 0 <= radial < cells_x:
            for component in range(parts):
                before, main, after = read(component, radial)
                around = jnp.where(sub < 4, after, before)
                known["raw", k, component] = jnp.concatenate([main, around], axis=0)


def inner_call(whole, row_shift):
    _, _, cells_x, cells_y, cells_z = whole.shape
    plans = handed_on(cells_x)

    def body(row_shift, whole, out):
        at = 0
        for row in range(cells_x):
            known = {}
            own_windows(whole, row, row_shift, known)
            values = Row(known)
            for key in plans[row][0]:
                out[at] = values.get(*key)
                at += 1

    vmem = pl.BlockSpec(memory_space=pltpu.VMEM)
    total = sum(len(plan[0]) for plan in plans)
    return pl.pallas_call(
        body,
        out_shape=jax.ShapeDtypeStruct((total, 2 * cells_y, cells_z), jnp.float32),
        in_specs=[pl.BlockSpec(memory_space=pltpu.SMEM), vmem],
        out_specs=vmem,
        compiler_params=pltpu.CompilerParams(vmem_limit_bytes=32 * 1024 * 1024),
        cost_estimate=pl.CostEstimate(flops=10**7, bytes_accessed=10**6, transcendentals=10**5),
        name="inner",
    )(row_shift, whole)


def load_stage(plans, level, ref, known):
    at = 0
    for row, plan in enumerate(plans):
        for key in plan[level]:
            known[row][key] = ref[at]
            at += 1


def middle_call(inner, from_above, cells_x):
    plans = handed_on(cells_x)

    def body(inner, from_above, out):
        known = [{} for _ in range(cells_x)]
        load_stage(plans, 0, inner, known)
        unpack(from_above, high_windows(cells_x), known)
        at = 0
        for row in range(cells_x):
            values = Row(known[row])
            for key in plans[row][1]:
                out[at] = values.get(*key)
                at += 1

    vmem = pl.BlockSpec(memory_space=pltpu.VMEM)
    total = sum(len(plan[1]) for plan in plans)
    return pl.pallas_call(
        body,
        out_shape=jax.ShapeDtypeStruct((total,) + inner.shape[1:], jnp.float32),
        in_specs=[vmem] * 2,
        out_specs=vmem,
        compiler_params=pltpu.CompilerParams(vmem_limit_bytes=32 * 1024 * 1024),
        cost_estimate=pl.CostEstimate(flops=10**6, bytes_accessed=10**6, transcendentals=10**4),
        name="middle",
    )(inner, from_above)


def outer_call(inner, middle, from_below, cells_x, parts):
    cells_y, cells_z = inner.shape[1] // 2, inner.shape[2]
    plans = handed_on(cells_x)

    def body(inner, middle, from_below, out):
        known = [{} for _ in range(cells_x)]
        load_stage(plans, 0, inner, known)
        load_stage(plans, 1, middle, known)
        unpack(from_below, low_windows(cells_x), known)
        for row in range(cells_x):
            values = Row(known[row])
            for component in range(parts):
                out[component, row] = values.get("out", component)[0:cells_y]

    vmem = pl.BlockSpec(memory_space=pltpu.VMEM)
    return pl.pallas_call(
        body,
        out_shape=jax.ShapeDtypeStruct((parts, cells_x, cells_y, cells_z), jnp.float32),
        in_specs=[vmem] * 3,
        out_specs=vmem,
        compiler_params=pltpu.CompilerParams(vmem_limit_bytes=32 * 1024 * 1024),
        name="outer",
    )(inner, middle, from_below)


def on_device(fields, shear_offset, row_shift):
    count_x, count_y = lax.axis_size("gx"), lax.axis_size("gy")
    upward = [(i, (i + 1) % count_x) for i in range(count_x)]
    downward = [(target, source) for source, target in upward]

    def other_core(values):
        return lax.ppermute(values, "gy", [(i, i ^ 1) for i in range(count_y)])

    own = jnp.roll(fields, fields.shape[0] // 2, axis=0)
    meet = []
    for x in range(count_x):
        for y in range(count_y):
            other = (x + 1 if (x + y) % 2 == 0 else x - 1) % count_x
            meet.append((x * count_y + y, other * count_y + y))
    received = lax.ppermute(row_shift, ("gx", "gy"), meet)
    swapped = other_core(received)
    near = [fields] + [
        lax.ppermute(fields, "gy", [(i, (i + step) % count_y) for i in range(count_y)])
        for step in range(2, count_y, 2)
    ]
    passed_on = list(near)
    middle = len(near) // 2
    passed_on[middle], received, swapped = lax.optimization_barrier(
        (near[middle], received, swapped)
    )
    far = [other_core(values) for values in passed_on]
    near[0] = own
    whole, to_above, to_below = windows_call(near, far, received, swapped, shear_offset)
    from_below = lax.ppermute(to_above, "gx", upward)
    from_above = lax.ppermute(to_below, "gx", downward)
    inner = inner_call(whole, row_shift)
    middle = middle_call(inner, from_above, fields.shape[1])
    return outer_call(inner, middle, from_below, fields.shape[1], fields.shape[0])


def solution(mesh):
    placed = (P(None, "gx", "gy", None), P(), P("gx"))
    return jax.shard_map(
        on_device, mesh=mesh, in_specs=placed, out_specs=P(None, "gx", "gy", None), check_vma=False
    )
```

time: 871 us -> 25.1 us (0.03)
  local copies, waits for them, and re-layouts: 795 us -> 0.83 us
  waiting for transfers between devices: 60.8 us -> 8.13 us
    gather x2 -> x0, local copies, waits for them, and re-layouts: 791 us -> none  [roll_loop(): return jnp.take_along_axis(united, positions, axis=row_axis)]
    ppermute x12 -> x11, waiting for transfers between devices: 60.8 us -> 8.13 us  [the longest x1 2.47 us: on_device(): from_above = lax.ppermute(to_below, 'gx', downward)]
  transfers between devices with their start and end apart: 12 -> 11, of which waited for: 11 -> 8; matrix products, arithmetic and copies ran while one was open for 0% -> 3% of each run, Pallas kernels for 0% -> 8%
where the time goes in v1:
time: 25.1 us; the launch traced here: 24.9 us
  starting transfers between devices  11.7 us (47%)
  waiting for transfers between devices  8.13 us (32%)
  Pallas kernels  3.52 us (14%)
  local copies, waits for them, and re-layouts  0.83 us (3%)
  between operations  0.69 us (3%)
    ppermute x3, starting transfers between devices, on_device(): lax.ppermute(fields, 'gy', [(i, (i + step) % count_y) for i in range(coun...  6.96 us
    ppermute x1, starting transfers between devices, on_device(): from_above = lax.ppermute(to_below, 'gx', downward)  2.5 us
    ppermute x1, waiting for transfers between devices, on_device(): from_above = lax.ppermute(to_below, 'gx', downward)  2.47 us
    ppermute x5, waiting for transfers between devices, other_core(): return lax.ppermute(values, 'gy', [(i, i ^ 1) for i in range(count_y)])  2.12 us
    ppermute x1, waiting for transfers between devices, on_device(): from_below = lax.ppermute(to_above, 'gx', upward)  2.07 us
    ppermute x1, starting transfers between devices, on_device(): received = lax.ppermute(row_shift, ('gx', 'gy'), meet)  1.49 us
    pallas_call x1, Pallas kernels, inner_call(): pl.pallas_call(body, out_shape=jax.ShapeDtypeStruct((total, 2 * cells_y,...  1.29 us
    pallas_call x1, Pallas kernels, outer_call(): pl.pallas_call(body, out_shape=jax.ShapeDtypeStruct((parts, cells_x, cell...  0.94 us
  transfers between devices with their start and end apart: 11, of which 8 were waited for; matrix products, arithmetic and copies ran while one was open for 3% of the time, Pallas kernels for 8%

profile of v1, /device:TPU:0, one launch (start us, length us, event | category | flops | bytes accessed | tf_op | source)
XLA Modules:
  0.0 24.9 jit_solution(16623241413692968713)
XLA Ops:
  0.0 3.0 %collective-permute-start.3 = (f32[8,3,8,128]{3,2,1,0:T(8,128)}, f32[8,3,8,128]{3,2,1,0:T(8,128)S(1)}, u32[]{:S(2)}, u32[]{:S(2)}) collective-permute-start(f32[8,3,8,128]{3,2,1,0:T(8,128)} %param.3), channel_id=1, source_target_pairs={{0,2},{1,3},{2,4},{3,5},{4,6},{5,7},{6,0},{7,1},{8,10},{9,11},{10,... | collective-permute-start | bytes 294920 | tf_op jit(solution)/shard_map/ppermute | solution.py:556
  3.0 2.6 %collective-permute-start = (f32[8,3,8,128]{3,2,1,0:T(8,128)}, f32[8,3,8,128]{3,2,1,0:T(8,128)S(1)}, u32[]{:S(2)}, u32[]{:S(2)}) collective-permute-start(f32[8,3,8,128]{3,2,1,0:T(8,128)} %param.3), channel_id=1, source_target_pairs={{0,4},{1,5},{2,6},{3,7},{4,0},{5,1},{6,2},{7,3},{8,12},{9,13},{10,... | collective-permute-start | bytes 294920 | tf_op jit(solution)/shard_map/ppermute | solution.py:556
  5.6 0.0 collective-permute-start.5
  5.6 1.3 %collective-permute-start.4 = (f32[8,3,8,128]{3,2,1,0:T(8,128)}, f32[8,3,8,128]{3,2,1,0:T(8,128)S(1)}, u32[]{:S(2)}, u32[]{:S(2)}) collective-permute-start(f32[8,3,8,128]{3,2,1,0:T(8,128)} %param.3), channel_id=1, source_target_pairs={{0,6},{1,7},{2,0},{3,1},{4,2},{5,3},{6,4},{7,5},{8,14},{9,15},{10,... | collective-permute-start | bytes 294920 | tf_op jit(solution)/shard_map/ppermute | solution.py:556
  7.0 1.5 %collective-permute-start.1 = (s32[3]{0:T(128)}, s32[3]{0:T(128)S(1)}, u32[]{:S(2)}, u32[]{:S(2)}) collective-permute-start(s32[3]{0:T(128)} %row_shift.1), channel_id=1, source_target_pairs={{0,8},{1,25},{2,10},{3,27},{4,12},{5,29},{6,14},{7,31},{8,0},{9,17... | collective-permute-start | bytes 44 | tf_op jit(solution)/shard_map/ppermute | solution.py:553
  8.5 0.8 %fusion = (f32[4,3,8,128]{3,2,1,0:T(8,128)S(1)}, f32[4,3,8,128]{3,2,1,0:T(8,128)S(1)}) fusion(f32[8,3,8,128]{3,2,1,0:T(8,128)} %param.3), kind=kLoop, calls=%fused_computation.1 | loop fusion | bytes 196608 | tf_op jit(solution)/shard_map/jit(_roll_static)/slice | solution.py:547
  9.9 0.7 %collective-permute-done.1.received = s32[3]{0:T(128)S(1)} collective-permute-done((s32[3]{0:T(128)}, s32[3]{0:T(128)S(1)}, u32[]{:S(2)}, u32[]{:S(2)}) %collective-permute-start.1) | collective-permute-done | bytes 44 | tf_op jit(solution)/shard_map/ppermute | solution.py:553
  10.6 0.3 %collective-permute-start.2 = (s32[3]{0:T(128)S(1)}, s32[3]{0:T(128)S(1)}, u32[]{:S(2)}, u32[]{:S(2)}) collective-permute-start(s32[3]{0:T(128)S(1)} %collective-permute-done.1.received), channel_id=1, source_target_pairs={{0,1},{1,0},{2,3},{3,2},{4,5},{5,4},{6,7},{7,6},{8,9},{9,8},{10,11... | collective-permute-start | bytes 44 | tf_op jit(solution)/shard_map/ppermute | solution.py:545
  10.9 0.8 %collective-permute-done.2.swapped = s32[3]{0:T(128)S(1)} collective-permute-done((s32[3]{0:T(128)S(1)}, s32[3]{0:T(128)S(1)}, u32[]{:S(2)}, u32[]{:S(2)}) %collective-permute-start.2) | collective-permute-done | bytes 44 | tf_op jit(solution)/shard_map/ppermute | solution.py:545
  11.8 0.6 %collective-permute-done.refs_2_ = f32[8,3,8,128]{3,2,1,0:T(8,128)S(1)} collective-permute-done((f32[8,3,8,128]{3,2,1,0:T(8,128)}, f32[8,3,8,128]{3,2,1,0:T(8,128)S(1)}, u32[]{:S(2)}, u32[]{:S(2)}) %collective-permute-start) | collective-permute-done | bytes 98336 | tf_op jit(solution)/shard_map/ppermute | solution.py:556
  12.4 0.0 collective-permute-start.7
  12.4 0.0 collective-permute-done.3.refs_1_
  12.4 0.5 %collective-permute-start.6 = (f32[8,3,8,128]{3,2,1,0:T(8,128)S(1)}, f32[8,3,8,128]{3,2,1,0:T(8,128)S(1)}, u32[]{:S(2)}, u32[]{:S(2)}) collective-permute-start(f32[8,3,8,128]{3,2,1,0:T(8,128)S(1)} %collective-permute-done.3.refs_1_), channel_id=1, source_target_pairs={{0,1},{1,0},{2,3},{3,2},{4,5},{5,4},{6,7},{7,6},{8,9},{9,8},{10,11... | collective-permute-start | bytes 294920 | tf_op jit(solution)/shard_map/ppermute | solution.py:545
  12.9 0.1 collective-permute-done.4.refs_3_
  13.0 0.0 collective-permute-start.8
  13.1 0.8 %collective-permute-done.6.refs_5_ = f32[8,3,8,128]{3,2,1,0:T(8,128)S(1)} collective-permute-done((f32[8,3,8,128]{3,2,1,0:T(8,128)S(1)}, f32[8,3,8,128]{3,2,1,0:T(8,128)S(1)}, u32[]{:S(2)}, u32[]{:S(2)}) %collective-permute-start.6) | collective-permute-done | bytes 98336 | tf_op jit(solution)/shard_map/ppermute | solution.py:545
  13.9 0.5 %collective-permute-done.8.refs_7_ = f32[8,3,8,128]{3,2,1,0:T(8,128)S(1)} collective-permute-done((f32[8,3,8,128]{3,2,1,0:T(8,128)S(1)}, f32[8,3,8,128]{3,2,1,0:T(8,128)S(1)}, u32[]{:S(2)}, u32[]{:S(2)}) %collective-permute-start.8) | collective-permute-done | bytes 98336 | tf_op jit(solution)/shard_map/ppermute | solution.py:545
  14.3 0.7 %windows.1 = (f32[8,8,3,8,128]{4,3,2,1,0:T(8,128)S(1)}, f32[28,8,128]{2,1,0:T(8,128)S(1)}, f32[31,8,128]{2,1,0:T(8,128)S(1)}) custom-call(s32[1]{0:T(128)S(6)} %copy.4.offset, s32[3]{0:T(128)S(1)} %collective-permute-done.1.received, s32[3]{0:T(128)S(1)} %collective-permute-done.2.swapped, f32[8,3,8,128]{3,2,1,0:T(8,128)S(1)} %pad_maximum_fusion.refs_0_, ...), custom_call_target="tpu_custom_call" | custom-call | tf_op jit(solution)/shard_map/windows/pallas_call | solution.py:364
  15.1 2.5 %collective-permute-start.9 = (f32[31,8,128]{2,1,0:T(8,128)S(1)}, f32[31,8,128]{2,1,0:T(8,128)S(1)}, u32[]{:S(2)}, u32[]{:S(2)}) collective-permute-start(f32[31,8,128]{2,1,0:T(8,128)S(1)} %get-tuple-element.15), channel_id=1, source_target_pairs={{8,0},{16,8},{24,16},{0,24},{9,1},{17,9},{25,17},{1,25},{10,2},{18... | collective-permute-start | bytes 380936 | tf_op jit(solution)/shard_map/ppermute | solution.py:568
  17.6 1.3 %inner.1 = f32[132,16,128]{2,1,0:T(8,128)S(1)} custom-call(s32[3]{0:T(128)S(1)} %copy-done, f32[8,8,3,8,128]{4,3,2,1,0:T(8,128)S(1)} %get-tuple-element.14.whole), custom_call_target="tpu_custom_call" | custom-call | flops 10000000 | bytes 1000000 | tf_op jit(solution)/shard_map/inner/pallas_call | solution.py:468
  18.8 2.5 %collective-permute-done.9.from_above = f32[31,8,128]{2,1,0:T(8,128)S(1)} collective-permute-done((f32[31,8,128]{2,1,0:T(8,128)S(1)}, f32[31,8,128]{2,1,0:T(8,128)S(1)}, u32[]{:S(2)}, u32[]{:S(2)}) %collective-permute-start.9) | collective-permute-done | bytes 127008 | tf_op jit(solution)/shard_map/ppermute | solution.py:568
  21.3 0.6 %middle.1 = f32[17,16,128]{2,1,0:T(8,128)S(1)} custom-call(f32[132,16,128]{2,1,0:T(8,128)S(1)} %inner.1, f32[31,8,128]{2,1,0:T(8,128)S(1)} %collective-permute-done.9.from_above), custom_call_target="tpu_custom_call" | custom-call | flops 1000000 | bytes 1000000 | tf_op jit(solution)/shard_map/middle/pallas_call | solution.py:503
  21.9 2.1 %collective-permute-done.10.from_below = f32[28,8,128]{2,1,0:T(8,128)S(1)} collective-permute-done((f32[28,8,128]{2,1,0:T(8,128)S(1)}, f32[28,8,128]{2,1,0:T(8,128)S(1)}, u32[]{:S(2)}, u32[]{:S(2)}) %collective-permute-start.10) | collective-permute-done | bytes 114720 | tf_op jit(solution)/shard_map/ppermute | solution.py:567
  24.0 0.9 %outer.1 = f32[8,3,8,128]{3,2,1,0:T(8,128)} custom-call(f32[132,16,128]{2,1,0:T(8,128)S(1)} %inner.1, f32[17,16,128]{2,1,0:T(8,128)S(1)} %middle.1, f32[28,8,128]{2,1,0:T(8,128)S(1)} %collective-permute-done.10.from_below), custom_call_target="tpu_custom_call" | custom-call | tf_op jit(solution)/shard_map/outer/pallas_call | solution.py:529
  (6 shorter events, 0.0 us)
Async XLA Ops:
  0.0 17.6 %copy-start = (s32[3]{0:T(128)S(1)}, s32[3]{0:T(128)}, u32[]{:S(2)}) copy-start(s32[3]{0:T(128)} %row_shift.1) | copy-start | bytes 40
  0.0 12.4 %collective-permute-start.3 = (f32[8,3,8,128]{3,2,1,0:T(8,128)}, f32[8,3,8,128]{3,2,1,0:T(8,128)S(1)}, u32[]{:S(2)}, u32[]{:S(2)}) collective-permute-start(f32[8,3,8,128]{3,2,1,0:T(8,128)} %param.3), channel_id=1, source_target_pairs={{0,2},{1,3},{2,4},{3,5},{4,6},{5,7},{6,0},{7,1},{8,10},{9,11},{10,... | collective-permute-start | bytes 294920 | tf_op jit(solution)/shard_map/ppermute | solution.py:556
  3.0 9.4 %collective-permute-start = (f32[8,3,8,128]{3,2,1,0:T(8,128)}, f32[8,3,8,128]{3,2,1,0:T(8,128)S(1)}, u32[]{:S(2)}, u32[]{:S(2)}) collective-permute-start(f32[8,3,8,128]{3,2,1,0:T(8,128)} %param.3), channel_id=1, source_target_pairs={{0,4},{1,5},{2,6},{3,7},{4,0},{5,1},{6,2},{7,3},{8,12},{9,13},{10,... | collective-permute-start | bytes 294920 | tf_op jit(solution)/shard_map/ppermute | solution.py:556
  5.6 7.4 %collective-permute-start.5 = (f32[8,3,8,128]{3,2,1,0:T(8,128)}, f32[8,3,8,128]{3,2,1,0:T(8,128)S(1)}, u32[]{:S(2)}, u32[]{:S(2)}) collective-permute-start(f32[8,3,8,128]{3,2,1,0:T(8,128)} %param.3), channel_id=1, source_target_pairs={{0,1},{1,0},{2,3},{3,2},{4,5},{5,4},{6,7},{7,6},{8,9},{9,8},{10,11... | collective-permute-start | bytes 294920 | tf_op jit(solution)/shard_map/ppermute | solution.py:545
  5.6 7.4 %collective-permute-start.4 = (f32[8,3,8,128]{3,2,1,0:T(8,128)}, f32[8,3,8,128]{3,2,1,0:T(8,128)S(1)}, u32[]{:S(2)}, u32[]{:S(2)}) collective-permute-start(f32[8,3,8,128]{3,2,1,0:T(8,128)} %param.3), channel_id=1, source_target_pairs={{0,6},{1,7},{2,0},{3,1},{4,2},{5,3},{6,4},{7,5},{8,14},{9,15},{10,... | collective-permute-start | bytes 294920 | tf_op jit(solution)/shard_map/ppermute | solution.py:556
  7.0 3.7 %collective-permute-start.1 = (s32[3]{0:T(128)}, s32[3]{0:T(128)S(1)}, u32[]{:S(2)}, u32[]{:S(2)}) collective-permute-start(s32[3]{0:T(128)} %row_shift.1), channel_id=1, source_target_pairs={{0,8},{1,25},{2,10},{3,27},{4,12},{5,29},{6,14},{7,31},{8,0},{9,17... | collective-permute-start | bytes 44 | tf_op jit(solution)/shard_map/ppermute | solution.py:553
  10.6 1.1 %collective-permute-start.2 = (s32[3]{0:T(128)S(1)}, s32[3]{0:T(128)S(1)}, u32[]{:S(2)}, u32[]{:S(2)}) collective-permute-start(s32[3]{0:T(128)S(1)} %collective-permute-done.1.received), channel_id=1, source_target_pairs={{0,1},{1,0},{2,3},{3,2},{4,5},{5,4},{6,7},{7,6},{8,9},{9,8},{10,11... | collective-permute-start | bytes 44 | tf_op jit(solution)/shard_map/ppermute | solution.py:545
  12.4 1.5 %collective-permute-start.7 = (f32[8,3,8,128]{3,2,1,0:T(8,128)S(1)}, f32[8,3,8,128]{3,2,1,0:T(8,128)S(1)}, u32[]{:S(2)}, u32[]{:S(2)}) collective-permute-start(f32[8,3,8,128]{3,2,1,0:T(8,128)S(1)} %collective-permute-done.refs_2_), channel_id=1, source_target_pairs={{0,1},{1,0},{2,3},{3,2},{4,5},{5,4},{6,7},{7,6},{8,9},{9,8},{10,11... | collective-permute-start | bytes 294920 | tf_op jit(solution)/shard_map/ppermute | solution.py:545
  12.4 1.5 %collective-permute-start.6 = (f32[8,3,8,128]{3,2,1,0:T(8,128)S(1)}, f32[8,3,8,128]{3,2,1,0:T(8,128)S(1)}, u32[]{:S(2)}, u32[]{:S(2)}) collective-permute-start(f32[8,3,8,128]{3,2,1,0:T(8,128)S(1)} %collective-permute-done.3.refs_1_), channel_id=1, source_target_pairs={{0,1},{1,0},{2,3},{3,2},{4,5},{5,4},{6,7},{7,6},{8,9},{9,8},{10,11... | collective-permute-start | bytes 294920 | tf_op jit(solution)/shard_map/ppermute | solution.py:545
  13.0 1.3 %collective-permute-start.8 = (f32[8,3,8,128]{3,2,1,0:T(8,128)S(1)}, f32[8,3,8,128]{3,2,1,0:T(8,128)S(1)}, u32[]{:S(2)}, u32[]{:S(2)}) collective-permute-start(f32[8,3,8,128]{3,2,1,0:T(8,128)S(1)} %collective-permute-done.4.refs_3_), channel_id=1, source_target_pairs={{0,1},{1,0},{2,3},{3,2},{4,5},{5,4},{6,7},{7,6},{8,9},{9,8},{10,11... | collective-permute-start | bytes 294920 | tf_op jit(solution)/shard_map/ppermute | solution.py:545
  15.1 6.3 %collective-permute-start.9 = (f32[31,8,128]{2,1,0:T(8,128)S(1)}, f32[31,8,128]{2,1,0:T(8,128)S(1)}, u32[]{:S(2)}, u32[]{:S(2)}) collective-permute-start(f32[31,8,128]{2,1,0:T(8,128)S(1)} %get-tuple-element.15), channel_id=1, source_target_pairs={{8,0},{16,8},{24,16},{0,24},{9,1},{17,9},{25,17},{1,25},{10,2},{18... | collective-permute-start | bytes 380936 | tf_op jit(solution)/shard_map/ppermute | solution.py:568
  17.6 6.4 %collective-permute-start.10 = (f32[28,8,128]{2,1,0:T(8,128)S(1)}, f32[28,8,128]{2,1,0:T(8,128)S(1)}, u32[]{:S(2)}, u32[]{:S(2)}) collective-permute-start(f32[28,8,128]{2,1,0:T(8,128)S(1)} %get-tuple-element.16), channel_id=1, source_target_pairs={{0,8},{8,16},{16,24},{24,0},{1,9},{9,17},{17,25},{25,1},{2,10},{10... | collective-permute-start | bytes 344072 | tf_op jit(solution)/shard_map/ppermute | solution.py:567

commit v2 on v1

--- a/solution.py
+++ b/solution.py
@@ -312,15 +312,20 @@
     lows, highs = low_windows(cells_x), high_windows(cells_x)
 
     def body(offset, received, swapped, *refs):
-        ins, whole, outs = refs[:blocks], refs[blocks], refs[blocks + 1 : -2]
-        shifts, sems = refs[-2:]
-        copies = [
-            pltpu.make_async_copy(source, shifts.at[at], sems.at[at])
-            for at, source in enumerate((received, swapped))
-        ]
-        for copy in copies:
-            copy.start()
+        ins, whole, outs = refs[:blocks], refs[blocks], refs[blocks + 1 :]
         place_x, place_y = lax.axis_index("gx"), lax.axis_index("gy")
+        here = remainder(place_x + place_y, 2) == 0
+        lane = lax.broadcasted_iota(jnp.int32, (1, cells_x), 1)
+        one, other = (
+            source[...].reshape(1, cells_x).astype(jnp.float32) for source in (received, swapped)
+        )
+
+        def scalars(values):
+            return [
+                jnp.sum(jnp.where(lane == i, values, 0.0)).astype(jnp.int32) for i in range(cells_x)
+            ]
+
+        above, below = scalars(jnp.where(here, one, other)), scalars(jnp.where(here, other, one))
         last = lax.axis_size("gx") - 1
         for side in range(2):
             for step in range(count):
@@ -332,13 +337,6 @@
                 else:
                     whole[place] = block[...]
         sub = lax.broadcasted_iota(jnp.int32, (cells_y, cells_z), 0)
-        for copy in copies:
-            copy.wait()
-        here = remainder(place_x + place_y, 2) == 0
-        above, below = (
-            [jnp.where(here, shifts[one, i], shifts[1 - one, i]) for i in range(cells_x)]
-            for one in range(2)
-        )
         for out, shift_by, wanted, end, sign, turn in (
             (outs[0], above, lows, last, 1, cells_x),
             (outs[1], below, highs, 0, -1, -cells_x),
@@ -370,7 +368,6 @@
         ],
         in_specs=[smem] + [vmem] * (2 + blocks),
         out_specs=[vmem] * 3,
-        scratch_shapes=[pltpu.SMEM((2, cells_x), jnp.int32), pltpu.SemaphoreType.DMA((2,))],
         compiler_params=pltpu.CompilerParams(vmem_limit_bytes=32 * 1024 * 1024),
         name="windows",
     )(offset, received, swapped, *near, *far)

time: 25.1 us -> 24.6 us (0.980)
  Pallas kernels: 3.52 us -> 3.08 us
    pallas_call x1, Pallas kernels: 0.7 us -> 0.25 us  [windows_call(): pl.pallas_call(body, out_shape=[jax.ShapeDtypeStruct((blocks, parts, cell...]
where the time goes in v2:
time: 24.6 us; the launch traced here: 24.5 us
  starting transfers between devices  11.7 us (48%)
  waiting for transfers between devices  8.13 us (33%)
  Pallas kernels  3.08 us (13%)
  local copies, waits for them, and re-layouts  0.83 us (3%)
  between operations  0.68 us (3%)
    ppermute x3, starting transfers between devices, on_device(): lax.ppermute(fields, 'gy', [(i, (i + step) % count_y) for i in range(coun...  6.96 us
    ppermute x1, starting transfers between devices, on_device(): from_above = lax.ppermute(to_below, 'gx', downward)  2.5 us
    ppermute x1, waiting for transfers between devices, on_device(): from_above = lax.ppermute(to_below, 'gx', downward)  2.47 us
    ppermute x5, waiting for transfers between devices, other_core(): return lax.ppermute(values, 'gy', [(i, i ^ 1) for i in range(count_y)])  2.12 us
    ppermute x1, waiting for transfers between devices, on_device(): from_below = lax.ppermute(to_above, 'gx', upward)  2.07 us
    ppermute x1, starting transfers between devices, on_device(): received = lax.ppermute(row_shift, ('gx', 'gy'), meet)  1.49 us
    pallas_call x1, Pallas kernels, inner_call(): pl.pallas_call(body, out_shape=jax.ShapeDtypeStruct((total, 2 * cells_y,...  1.29 us
    pallas_call x1, Pallas kernels, outer_call(): pl.pallas_call(body, out_shape=jax.ShapeDtypeStruct((parts, cells_x, cell...  0.94 us
  transfers between devices with their start and end apart: 11, of which 8 were waited for; matrix products, arithmetic and copies ran while one was open for 3% of the time, Pallas kernels for 8%

profile of v2, /device:TPU:0, one launch (start us, length us, event | category | flops | bytes accessed | tf_op | source)
XLA Modules:
  0.0 24.5 jit_solution(12427911703882057801)
XLA Ops:
  0.0 3.0 %collective-permute-start.3 = (f32[8,3,8,128]{3,2,1,0:T(8,128)}, f32[8,3,8,128]{3,2,1,0:T(8,128)S(1)}, u32[]{:S(2)}, u32[]{:S(2)}) collective-permute-start(f32[8,3,8,128]{3,2,1,0:T(8,128)} %param.3), channel_id=1, source_target_pairs={{0,2},{1,3},{2,4},{3,5},{4,6},{5,7},{6,0},{7,1},{8,10},{9,11},{10,... | collective-permute-start | bytes 294920 | tf_op jit(solution)/shard_map/ppermute | solution.py:553
  3.0 2.6 %collective-permute-start = (f32[8,3,8,128]{3,2,1,0:T(8,128)}, f32[8,3,8,128]{3,2,1,0:T(8,128)S(1)}, u32[]{:S(2)}, u32[]{:S(2)}) collective-permute-start(f32[8,3,8,128]{3,2,1,0:T(8,128)} %param.3), channel_id=1, source_target_pairs={{0,4},{1,5},{2,6},{3,7},{4,0},{5,1},{6,2},{7,3},{8,12},{9,13},{10,... | collective-permute-start | bytes 294920 | tf_op jit(solution)/shard_map/ppermute | solution.py:553
  5.6 0.0 collective-permute-start.5
  5.6 1.3 %collective-permute-start.4 = (f32[8,3,8,128]{3,2,1,0:T(8,128)}, f32[8,3,8,128]{3,2,1,0:T(8,128)S(1)}, u32[]{:S(2)}, u32[]{:S(2)}) collective-permute-start(f32[8,3,8,128]{3,2,1,0:T(8,128)} %param.3), channel_id=1, source_target_pairs={{0,6},{1,7},{2,0},{3,1},{4,2},{5,3},{6,4},{7,5},{8,14},{9,15},{10,... | collective-permute-start | bytes 294920 | tf_op jit(solution)/shard_map/ppermute | solution.py:553
  7.0 1.5 %collective-permute-start.1 = (s32[3]{0:T(128)}, s32[3]{0:T(128)S(1)}, u32[]{:S(2)}, u32[]{:S(2)}) collective-permute-start(s32[3]{0:T(128)} %row_shift.1), channel_id=1, source_target_pairs={{0,8},{1,25},{2,10},{3,27},{4,12},{5,29},{6,14},{7,31},{8,0},{9,17... | collective-permute-start | bytes 44 | tf_op jit(solution)/shard_map/ppermute | solution.py:550
  8.5 0.8 %fusion = (f32[4,3,8,128]{3,2,1,0:T(8,128)S(1)}, f32[4,3,8,128]{3,2,1,0:T(8,128)S(1)}) fusion(f32[8,3,8,128]{3,2,1,0:T(8,128)} %param.3), kind=kLoop, calls=%fused_computation.1 | loop fusion | bytes 196608 | tf_op jit(solution)/shard_map/jit(_roll_static)/slice | solution.py:544
  9.9 0.7 %collective-permute-done.1.received = s32[3]{0:T(128)S(1)} collective-permute-done((s32[3]{0:T(128)}, s32[3]{0:T(128)S(1)}, u32[]{:S(2)}, u32[]{:S(2)}) %collective-permute-start.1) | collective-permute-done | bytes 44 | tf_op jit(solution)/shard_map/ppermute | solution.py:550
  10.6 0.3 %collective-permute-start.2 = (s32[3]{0:T(128)S(1)}, s32[3]{0:T(128)S(1)}, u32[]{:S(2)}, u32[]{:S(2)}) collective-permute-start(s32[3]{0:T(128)S(1)} %collective-permute-done.1.received), channel_id=1, source_target_pairs={{0,1},{1,0},{2,3},{3,2},{4,5},{5,4},{6,7},{7,6},{8,9},{9,8},{10,11... | collective-permute-start | bytes 44 | tf_op jit(solution)/shard_map/ppermute | solution.py:542
  10.9 0.8 %collective-permute-done.2.swapped = s32[3]{0:T(128)S(1)} collective-permute-done((s32[3]{0:T(128)S(1)}, s32[3]{0:T(128)S(1)}, u32[]{:S(2)}, u32[]{:S(2)}) %collective-permute-start.2) | collective-permute-done | bytes 44 | tf_op jit(solution)/shard_map/ppermute | solution.py:542
  11.8 0.6 %collective-permute-done.refs_2_ = f32[8,3,8,128]{3,2,1,0:T(8,128)S(1)} collective-permute-done((f32[8,3,8,128]{3,2,1,0:T(8,128)}, f32[8,3,8,128]{3,2,1,0:T(8,128)S(1)}, u32[]{:S(2)}, u32[]{:S(2)}) %collective-permute-start) | collective-permute-done | bytes 98336 | tf_op jit(solution)/shard_map/ppermute | solution.py:553
  12.4 0.0 collective-permute-start.7
  12.4 0.0 collective-permute-done.3.refs_1_
  12.4 0.5 %collective-permute-start.6 = (f32[8,3,8,128]{3,2,1,0:T(8,128)S(1)}, f32[8,3,8,128]{3,2,1,0:T(8,128)S(1)}, u32[]{:S(2)}, u32[]{:S(2)}) collective-permute-start(f32[8,3,8,128]{3,2,1,0:T(8,128)S(1)} %collective-permute-done.3.refs_1_), channel_id=1, source_target_pairs={{0,1},{1,0},{2,3},{3,2},{4,5},{5,4},{6,7},{7,6},{8,9},{9,8},{10,11... | collective-permute-start | bytes 294920 | tf_op jit(solution)/shard_map/ppermute | solution.py:542
  12.9 0.1 collective-permute-done.4.refs_3_
  13.0 0.0 collective-permute-start.8
  13.1 0.8 %collective-permute-done.6.refs_5_ = f32[8,3,8,128]{3,2,1,0:T(8,128)S(1)} collective-permute-done((f32[8,3,8,128]{3,2,1,0:T(8,128)S(1)}, f32[8,3,8,128]{3,2,1,0:T(8,128)S(1)}, u32[]{:S(2)}, u32[]{:S(2)}) %collective-permute-start.6) | collective-permute-done | bytes 98336 | tf_op jit(solution)/shard_map/ppermute | solution.py:542
  13.9 0.5 %collective-permute-done.8.refs_7_ = f32[8,3,8,128]{3,2,1,0:T(8,128)S(1)} collective-permute-done((f32[8,3,8,128]{3,2,1,0:T(8,128)S(1)}, f32[8,3,8,128]{3,2,1,0:T(8,128)S(1)}, u32[]{:S(2)}, u32[]{:S(2)}) %collective-permute-start.8) | collective-permute-done | bytes 98336 | tf_op jit(solution)/shard_map/ppermute | solution.py:542
  14.3 0.3 %windows.1 = (f32[8,8,3,8,128]{4,3,2,1,0:T(8,128)S(1)}, f32[28,8,128]{2,1,0:T(8,128)S(1)}, f32[31,8,128]{2,1,0:T(8,128)S(1)}) custom-call(s32[1]{0:T(128)S(6)} %copy.4.offset, s32[3]{0:T(128)S(1)} %collective-permute-done.1.received, s32[3]{0:T(128)S(1)} %collective-permute-done.2.swapped, f32[8,3,8,128]{3,2,1,0:T(8,128)S(1)} %pad_maximum_fusion.refs_0_, ...), custom_call_target="tpu_custom_call" | custom-call | tf_op jit(solution)/shard_map/windows/pallas_call | solution.py:362
  14.6 2.5 %collective-permute-start.9 = (f32[31,8,128]{2,1,0:T(8,128)S(1)}, f32[31,8,128]{2,1,0:T(8,128)S(1)}, u32[]{:S(2)}, u32[]{:S(2)}) collective-permute-start(f32[31,8,128]{2,1,0:T(8,128)S(1)} %get-tuple-element.15), channel_id=1, source_target_pairs={{8,0},{16,8},{24,16},{0,24},{9,1},{17,9},{25,17},{1,25},{10,2},{18... | collective-permute-start | bytes 380936 | tf_op jit(solution)/shard_map/ppermute | solution.py:565
  17.1 1.3 %inner.1 = f32[132,16,128]{2,1,0:T(8,128)S(1)} custom-call(s32[3]{0:T(128)S(1)} %copy-done, f32[8,8,3,8,128]{4,3,2,1,0:T(8,128)S(1)} %get-tuple-element.14.whole), custom_call_target="tpu_custom_call" | custom-call | flops 10000000 | bytes 1000000 | tf_op jit(solution)/shard_map/inner/pallas_call | solution.py:465
  18.4 2.5 %collective-permute-done.9.from_above = f32[31,8,128]{2,1,0:T(8,128)S(1)} collective-permute-done((f32[31,8,128]{2,1,0:T(8,128)S(1)}, f32[31,8,128]{2,1,0:T(8,128)S(1)}, u32[]{:S(2)}, u32[]{:S(2)}) %collective-permute-start.9) | collective-permute-done | bytes 127008 | tf_op jit(solution)/shard_map/ppermute | solution.py:565
  20.9 0.6 %middle.1 = f32[17,16,128]{2,1,0:T(8,128)S(1)} custom-call(f32[132,16,128]{2,1,0:T(8,128)S(1)} %inner.1, f32[31,8,128]{2,1,0:T(8,128)S(1)} %collective-permute-done.9.from_above), custom_call_target="tpu_custom_call" | custom-call | flops 1000000 | bytes 1000000 | tf_op jit(solution)/shard_map/middle/pallas_call | solution.py:500
  21.5 2.1 %collective-permute-done.10.from_below = f32[28,8,128]{2,1,0:T(8,128)S(1)} collective-permute-done((f32[28,8,128]{2,1,0:T(8,128)S(1)}, f32[28,8,128]{2,1,0:T(8,128)S(1)}, u32[]{:S(2)}, u32[]{:S(2)}) %collective-permute-start.10) | collective-permute-done | bytes 114720 | tf_op jit(solution)/shard_map/ppermute | solution.py:564
  23.5 0.9 %outer.1 = f32[8,3,8,128]{3,2,1,0:T(8,128)} custom-call(f32[132,16,128]{2,1,0:T(8,128)S(1)} %inner.1, f32[17,16,128]{2,1,0:T(8,128)S(1)} %middle.1, f32[28,8,128]{2,1,0:T(8,128)S(1)} %collective-permute-done.10.from_below), custom_call_target="tpu_custom_call" | custom-call | tf_op jit(solution)/shard_map/outer/pallas_call | solution.py:526
  (6 shorter events, 0.0 us)
Async XLA Ops:
  0.0 17.1 %copy-start = (s32[3]{0:T(128)S(1)}, s32[3]{0:T(128)}, u32[]{:S(2)}) copy-start(s32[3]{0:T(128)} %row_shift.1) | copy-start | bytes 40
  0.0 12.4 %collective-permute-start.3 = (f32[8,3,8,128]{3,2,1,0:T(8,128)}, f32[8,3,8,128]{3,2,1,0:T(8,128)S(1)}, u32[]{:S(2)}, u32[]{:S(2)}) collective-permute-start(f32[8,3,8,128]{3,2,1,0:T(8,128)} %param.3), channel_id=1, source_target_pairs={{0,2},{1,3},{2,4},{3,5},{4,6},{5,7},{6,0},{7,1},{8,10},{9,11},{10,... | collective-permute-start | bytes 294920 | tf_op jit(solution)/shard_map/ppermute | solution.py:553
  3.0 9.4 %collective-permute-start = (f32[8,3,8,128]{3,2,1,0:T(8,128)}, f32[8,3,8,128]{3,2,1,0:T(8,128)S(1)}, u32[]{:S(2)}, u32[]{:S(2)}) collective-permute-start(f32[8,3,8,128]{3,2,1,0:T(8,128)} %param.3), channel_id=1, source_target_pairs={{0,4},{1,5},{2,6},{3,7},{4,0},{5,1},{6,2},{7,3},{8,12},{9,13},{10,... | collective-permute-start | bytes 294920 | tf_op jit(solution)/shard_map/ppermute | solution.py:553
  5.6 7.4 %collective-permute-start.5 = (f32[8,3,8,128]{3,2,1,0:T(8,128)}, f32[8,3,8,128]{3,2,1,0:T(8,128)S(1)}, u32[]{:S(2)}, u32[]{:S(2)}) collective-permute-start(f32[8,3,8,128]{3,2,1,0:T(8,128)} %param.3), channel_id=1, source_target_pairs={{0,1},{1,0},{2,3},{3,2},{4,5},{5,4},{6,7},{7,6},{8,9},{9,8},{10,11... | collective-permute-start | bytes 294920 | tf_op jit(solution)/shard_map/ppermute | solution.py:542
  5.6 7.4 %collective-permute-start.4 = (f32[8,3,8,128]{3,2,1,0:T(8,128)}, f32[8,3,8,128]{3,2,1,0:T(8,128)S(1)}, u32[]{:S(2)}, u32[]{:S(2)}) collective-permute-start(f32[8,3,8,128]{3,2,1,0:T(8,128)} %param.3), channel_id=1, source_target_pairs={{0,6},{1,7},{2,0},{3,1},{4,2},{5,3},{6,4},{7,5},{8,14},{9,15},{10,... | collective-permute-start | bytes 294920 | tf_op jit(solution)/shard_map/ppermute | solution.py:553
  7.0 3.7 %collective-permute-start.1 = (s32[3]{0:T(128)}, s32[3]{0:T(128)S(1)}, u32[]{:S(2)}, u32[]{:S(2)}) collective-permute-start(s32[3]{0:T(128)} %row_shift.1), channel_id=1, source_target_pairs={{0,8},{1,25},{2,10},{3,27},{4,12},{5,29},{6,14},{7,31},{8,0},{9,17... | collective-permute-start | bytes 44 | tf_op jit(solution)/shard_map/ppermute | solution.py:550
  10.6 1.1 %collective-permute-start.2 = (s32[3]{0:T(128)S(1)}, s32[3]{0:T(128)S(1)}, u32[]{:S(2)}, u32[]{:S(2)}) collective-permute-start(s32[3]{0:T(128)S(1)} %collective-permute-done.1.received), channel_id=1, source_target_pairs={{0,1},{1,0},{2,3},{3,2},{4,5},{5,4},{6,7},{7,6},{8,9},{9,8},{10,11... | collective-permute-start | bytes 44 | tf_op jit(solution)/shard_map/ppermute | solution.py:542
  12.4 1.5 %collective-permute-start.7 = (f32[8,3,8,128]{3,2,1,0:T(8,128)S(1)}, f32[8,3,8,128]{3,2,1,0:T(8,128)S(1)}, u32[]{:S(2)}, u32[]{:S(2)}) collective-permute-start(f32[8,3,8,128]{3,2,1,0:T(8,128)S(1)} %collective-permute-done.refs_2_), channel_id=1, source_target_pairs={{0,1},{1,0},{2,3},{3,2},{4,5},{5,4},{6,7},{7,6},{8,9},{9,8},{10,11... | collective-permute-start | bytes 294920 | tf_op jit(solution)/shard_map/ppermute | solution.py:542
  12.4 1.5 %collective-permute-start.6 = (f32[8,3,8,128]{3,2,1,0:T(8,128)S(1)}, f32[8,3,8,128]{3,2,1,0:T(8,128)S(1)}, u32[]{:S(2)}, u32[]{:S(2)}) collective-permute-start(f32[8,3,8,128]{3,2,1,0:T(8,128)S(1)} %collective-permute-done.3.refs_1_), channel_id=1, source_target_pairs={{0,1},{1,0},{2,3},{3,2},{4,5},{5,4},{6,7},{7,6},{8,9},{9,8},{10,11... | collective-permute-start | bytes 294920 | tf_op jit(solution)/shard_map/ppermute | solution.py:542
  13.0 1.3 %collective-permute-start.8 = (f32[8,3,8,128]{3,2,1,0:T(8,128)S(1)}, f32[8,3,8,128]{3,2,1,0:T(8,128)S(1)}, u32[]{:S(2)}, u32[]{:S(2)}) collective-permute-start(f32[8,3,8,128]{3,2,1,0:T(8,128)S(1)} %collective-permute-done.4.refs_3_), channel_id=1, source_target_pairs={{0,1},{1,0},{2,3},{3,2},{4,5},{5,4},{6,7},{7,6},{8,9},{9,8},{10,11... | collective-permute-start | bytes 294920 | tf_op jit(solution)/shard_map/ppermute | solution.py:542
  14.6 6.3 %collective-permute-start.9 = (f32[31,8,128]{2,1,0:T(8,128)S(1)}, f32[31,8,128]{2,1,0:T(8,128)S(1)}, u32[]{:S(2)}, u32[]{:S(2)}) collective-permute-start(f32[31,8,128]{2,1,0:T(8,128)S(1)} %get-tuple-element.15), channel_id=1, source_target_pairs={{8,0},{16,8},{24,16},{0,24},{9,1},{17,9},{25,17},{1,25},{10,2},{18... | collective-permute-start | bytes 380936 | tf_op jit(solution)/shard_map/ppermute | solution.py:565
  17.1 6.4 %collective-permute-start.10 = (f32[28,8,128]{2,1,0:T(8,128)S(1)}, f32[28,8,128]{2,1,0:T(8,128)S(1)}, u32[]{:S(2)}, u32[]{:S(2)}) collective-permute-start(f32[28,8,128]{2,1,0:T(8,128)S(1)} %get-tuple-element.16), channel_id=1, source_target_pairs={{0,8},{8,16},{16,24},{24,0},{1,9},{9,17},{17,25},{25,1},{2,10},{10... | collective-permute-start | bytes 344072 | tf_op jit(solution)/shard_map/ppermute | solution.py:564

commit v3 on v2

--- a/solution.py
+++ b/solution.py
@@ -548,17 +548,18 @@
             other = (x + 1 if (x + y) % 2 == 0 else x - 1) % count_x
             meet.append((x * count_y + y, other * count_y + y))
     received = lax.ppermute(row_shift, ("gx", "gy"), meet)
+    received, own = lax.optimization_barrier((received, own))
     swapped = other_core(received)
     near = [fields] + [
         lax.ppermute(fields, "gy", [(i, (i + step) % count_y) for i in range(count_y)])
         for step in range(2, count_y, 2)
     ]
     passed_on = list(near)
-    middle = len(near) // 2
-    passed_on[middle], received, swapped = lax.optimization_barrier(
-        (near[middle], received, swapped)
-    )
-    far = [other_core(values) for values in passed_on]
+    far = [other_core(near[0]), other_core(near[1])]
+    passed_on[2], received, swapped, _ = lax.optimization_barrier((near[2], received, swapped, far[1]))
+    far.append(other_core(passed_on[2]))
+    passed_on[3], _ = lax.optimization_barrier((near[3], passed_on[2]))
+    far += [other_core(values) for values in passed_on[3:]]
     near[0] = own
     whole, to_above, to_below = windows_call(near, far, received, swapped, shear_offset)
     from_below = lax.ppermute(to_above, "gx", upward)

time: 24.6 us -> 24.6 us (level)
  starting transfers between devices: 11.7 us -> 12.2 us
  waiting for transfers between devices: 8.13 us -> 7.67 us
    ppermute x5, waiting for transfers between devices: 2.12 us -> 1.48 us  [other_core(): return lax.ppermute(values, 'gy', [(i, i ^ 1) for i in range(count_y)])]
    ppermute x3, waiting for transfers between devices: 0.77 us -> 1.28 us  [on_device(): lax.ppermute(fields, 'gy', [(i, (i + step) % count_y) for i in range(coun...]
    ppermute x5, starting transfers between devices: 0.79 us -> 1.25 us  [other_core(): return lax.ppermute(values, 'gy', [(i, i ^ 1) for i in range(count_y)])]
    ppermute x1, waiting for transfers between devices: 0.7 us -> 0.37 us  [on_device(): received = lax.ppermute(row_shift, ('gx', 'gy'), meet)]
  transfers between devices with their start and end apart: 11 -> 11, of which waited for: 8 -> 7; matrix products, arithmetic and copies ran while one was open for 3% -> 3% of each run, Pallas kernels for 8% -> 8%
where the time goes in v3:
time: 24.6 us; the launch traced here: 24.5 us
  starting transfers between devices  12.2 us (50%)
  waiting for transfers between devices  7.67 us (31%)
  Pallas kernels  3.08 us (13%)
  local copies, waits for them, and re-layouts  0.83 us (3%)
  between operations  0.69 us (3%)
    ppermute x3, starting transfers between devices, on_device(): lax.ppermute(fields, 'gy', [(i, (i + step) % count_y) for i in range(coun...  6.96 us
    ppermute x1, starting transfers between devices, on_device(): from_above = lax.ppermute(to_below, 'gx', downward)  2.5 us
    ppermute x1, waiting for transfers between devices, on_device(): from_above = lax.ppermute(to_below, 'gx', downward)  2.47 us
    ppermute x1, waiting for transfers between devices, on_device(): from_below = lax.ppermute(to_above, 'gx', upward)  2.07 us
    ppermute x1, starting transfers between devices, on_device(): received = lax.ppermute(row_shift, ('gx', 'gy'), meet)  1.49 us
    ppermute x5, waiting for transfers between devices, other_core(): return lax.ppermute(values, 'gy', [(i, i ^ 1) for i in range(count_y)])  1.48 us
    pallas_call x1, Pallas kernels, inner_call(): pl.pallas_call(body, out_shape=jax.ShapeDtypeStruct((total, 2 * cells_y,...  1.29 us
    ppermute x3, waiting for transfers between devices, on_device(): lax.ppermute(fields, 'gy', [(i, (i + step) % count_y) for i in range(coun...  1.28 us
  transfers between devices with their start and end apart: 11, of which 7 were waited for; matrix products, arithmetic and copies ran while one was open for 3% of the time, Pallas kernels for 8%

profile of v3, /device:TPU:0, one launch (start us, length us, event | category | flops | bytes accessed | tf_op | source)
XLA Modules:
  0.0 24.5 jit_solution(17418341636714132885)
XLA Ops:
  0.0 3.0 %collective-permute-start.3 = (f32[8,3,8,128]{3,2,1,0:T(8,128)}, f32[8,3,8,128]{3,2,1,0:T(8,128)S(1)}, u32[]{:S(2)}, u32[]{:S(2)}) collective-permute-start(f32[8,3,8,128]{3,2,1,0:T(8,128)} %param.3), channel_id=1, source_target_pairs={{0,2},{1,3},{2,4},{3,5},{4,6},{5,7},{6,0},{7,1},{8,10},{9,11},{10,... | collective-permute-start | bytes 294920 | tf_op jit(solution)/shard_map/ppermute | solution.py:554
  3.0 2.6 %collective-permute-start = (f32[8,3,8,128]{3,2,1,0:T(8,128)}, f32[8,3,8,128]{3,2,1,0:T(8,128)S(1)}, u32[]{:S(2)}, u32[]{:S(2)}) collective-permute-start(f32[8,3,8,128]{3,2,1,0:T(8,128)} %param.3), channel_id=1, source_target_pairs={{0,4},{1,5},{2,6},{3,7},{4,0},{5,1},{6,2},{7,3},{8,12},{9,13},{10,... | collective-permute-start | bytes 294920 | tf_op jit(solution)/shard_map/ppermute | solution.py:554
  5.6 0.0 collective-permute-start.6
  5.6 1.3 %collective-permute-start.5 = (f32[8,3,8,128]{3,2,1,0:T(8,128)}, f32[8,3,8,128]{3,2,1,0:T(8,128)S(1)}, u32[]{:S(2)}, u32[]{:S(2)}) collective-permute-start(f32[8,3,8,128]{3,2,1,0:T(8,128)} %param.3), channel_id=1, source_target_pairs={{0,6},{1,7},{2,0},{3,1},{4,2},{5,3},{6,4},{7,5},{8,14},{9,15},{10,... | collective-permute-start | bytes 294920 | tf_op jit(solution)/shard_map/ppermute | solution.py:554
  7.0 1.5 %collective-permute-start.1 = (s32[3]{0:T(128)}, s32[3]{0:T(128)S(1)}, u32[]{:S(2)}, u32[]{:S(2)}) collective-permute-start(s32[3]{0:T(128)} %row_shift.1), channel_id=1, source_target_pairs={{0,8},{1,25},{2,10},{3,27},{4,12},{5,29},{6,14},{7,31},{8,0},{9,17... | collective-permute-start | bytes 44 | tf_op jit(solution)/shard_map/ppermute | solution.py:550
  8.5 0.8 %fusion = (f32[4,3,8,128]{3,2,1,0:T(8,128)S(1)}, f32[4,3,8,128]{3,2,1,0:T(8,128)S(1)}) fusion(f32[8,3,8,128]{3,2,1,0:T(8,128)} %param.3), kind=kLoop, calls=%fused_computation.1 | loop fusion | bytes 196608 | tf_op jit(solution)/shard_map/jit(_roll_static)/slice | solution.py:544
  9.3 0.0 collective-permute-done.3.refs_1_
  9.3 1.0 %collective-permute-start.4 = (f32[8,3,8,128]{3,2,1,0:T(8,128)S(1)}, f32[8,3,8,128]{3,2,1,0:T(8,128)S(1)}, u32[]{:S(2)}, u32[]{:S(2)}) collective-permute-start(f32[8,3,8,128]{3,2,1,0:T(8,128)S(1)} %collective-permute-done.3.refs_1_), channel_id=1, source_target_pairs={{0,1},{1,0},{2,3},{3,2},{4,5},{5,4},{6,7},{7,6},{8,9},{9,8},{10,11... | collective-permute-start | bytes 294920 | tf_op jit(solution)/shard_map/ppermute | solution.py:542
  10.3 0.4 %collective-permute-done.1.received = s32[3]{0:T(128)S(1)} collective-permute-done((s32[3]{0:T(128)}, s32[3]{0:T(128)S(1)}, u32[]{:S(2)}, u32[]{:S(2)}) %collective-permute-start.1) | collective-permute-done | bytes 44 | tf_op jit(solution)/shard_map/ppermute | solution.py:550
  10.6 0.3 %collective-permute-start.2 = (s32[3]{0:T(128)S(1)}, s32[3]{0:T(128)S(1)}, u32[]{:S(2)}, u32[]{:S(2)}) collective-permute-start(s32[3]{0:T(128)S(1)} %collective-permute-done.1.received), channel_id=1, source_target_pairs={{0,1},{1,0},{2,3},{3,2},{4,5},{5,4},{6,7},{7,6},{8,9},{9,8},{10,11... | collective-permute-start | bytes 44 | tf_op jit(solution)/shard_map/ppermute | solution.py:542
  10.9 0.8 %collective-permute-done.2.swapped = s32[3]{0:T(128)S(1)} collective-permute-done((s32[3]{0:T(128)S(1)}, s32[3]{0:T(128)S(1)}, u32[]{:S(2)}, u32[]{:S(2)}) %collective-permute-start.2) | collective-permute-done | bytes 44 | tf_op jit(solution)/shard_map/ppermute | solution.py:542
  11.8 0.6 %collective-permute-done.refs_2_ = f32[8,3,8,128]{3,2,1,0:T(8,128)S(1)} collective-permute-done((f32[8,3,8,128]{3,2,1,0:T(8,128)}, f32[8,3,8,128]{3,2,1,0:T(8,128)S(1)}, u32[]{:S(2)}, u32[]{:S(2)}) %collective-permute-start) | collective-permute-done | bytes 98336 | tf_op jit(solution)/shard_map/ppermute | solution.py:554
  12.4 0.0 collective-permute-done.4.refs_5_
  12.4 0.6 %collective-permute-done.5.refs_3_ = f32[8,3,8,128]{3,2,1,0:T(8,128)S(1)} collective-permute-done((f32[8,3,8,128]{3,2,1,0:T(8,128)}, f32[8,3,8,128]{3,2,1,0:T(8,128)S(1)}, u32[]{:S(2)}, u32[]{:S(2)}) %collective-permute-start.5) | collective-permute-done | bytes 98336 | tf_op jit(solution)/shard_map/ppermute | solution.py:554
  13.7 0.0 collective-permute-done.7.refs_6_
  13.7 0.6 %collective-permute-done.8.refs_7_ = f32[8,3,8,128]{3,2,1,0:T(8,128)S(1)} collective-permute-done((f32[8,3,8,128]{3,2,1,0:T(8,128)S(1)}, f32[8,3,8,128]{3,2,1,0:T(8,128)S(1)}, u32[]{:S(2)}, u32[]{:S(2)}) %collective-permute-start.8) | collective-permute-done | bytes 98336 | tf_op jit(solution)/shard_map/ppermute | solution.py:542
  14.3 0.3 %windows.1 = (f32[8,8,3,8,128]{4,3,2,1,0:T(8,128)S(1)}, f32[28,8,128]{2,1,0:T(8,128)S(1)}, f32[31,8,128]{2,1,0:T(8,128)S(1)}) custom-call(s32[1]{0:T(128)S(6)} %copy.4.offset, s32[3]{0:T(128)S(1)} %collective-permute-done.1.received, s32[3]{0:T(128)S(1)} %collective-permute-done.2.swapped, f32[8,3,8,128]{3,2,1,0:T(8,128)S(1)} %pad_maximum_fusion.refs_0_, ...), custom_call_target="tpu_custom_call" | custom-call | tf_op jit(solution)/shard_map/windows/pallas_call | solution.py:362
  14.6 2.5 %collective-permute-start.9 = (f32[31,8,128]{2,1,0:T(8,128)S(1)}, f32[31,8,128]{2,1,0:T(8,128)S(1)}, u32[]{:S(2)}, u32[]{:S(2)}) collective-permute-start(f32[31,8,128]{2,1,0:T(8,128)S(1)} %get-tuple-element.21), channel_id=1, source_target_pairs={{8,0},{16,8},{24,16},{0,24},{9,1},{17,9},{25,17},{1,25},{10,2},{18... | collective-permute-start | bytes 380936 | tf_op jit(solution)/shard_map/ppermute | solution.py:566
  17.1 0.0 collective-permute-start.10
  17.1 1.3 %inner.1 = f32[132,16,128]{2,1,0:T(8,128)S(1)} custom-call(s32[3]{0:T(128)S(1)} %copy-done, f32[8,8,3,8,128]{4,3,2,1,0:T(8,128)S(1)} %get-tuple-element.20.whole), custom_call_target="tpu_custom_call" | custom-call | flops 10000000 | bytes 1000000 | tf_op jit(solution)/shard_map/inner/pallas_call | solution.py:465
  18.4 2.5 %collective-permute-done.9.from_above = f32[31,8,128]{2,1,0:T(8,128)S(1)} collective-permute-done((f32[31,8,128]{2,1,0:T(8,128)S(1)}, f32[31,8,128]{2,1,0:T(8,128)S(1)}, u32[]{:S(2)}, u32[]{:S(2)}) %collective-permute-start.9) | collective-permute-done | bytes 127008 | tf_op jit(solution)/shard_map/ppermute | solution.py:566
  20.9 0.6 %middle.1 = f32[17,16,128]{2,1,0:T(8,128)S(1)} custom-call(f32[132,16,128]{2,1,0:T(8,128)S(1)} %inner.1, f32[31,8,128]{2,1,0:T(8,128)S(1)} %collective-permute-done.9.from_above), custom_call_target="tpu_custom_call" | custom-call | flops 1000000 | bytes 1000000 | tf_op jit(solution)/shard_map/middle/pallas_call | solution.py:500
  21.5 2.1 %collective-permute-done.10.from_below = f32[28,8,128]{2,1,0:T(8,128)S(1)} collective-permute-done((f32[28,8,128]{2,1,0:T(8,128)S(1)}, f32[28,8,128]{2,1,0:T(8,128)S(1)}, u32[]{:S(2)}, u32[]{:S(2)}) %collective-permute-start.10) | collective-permute-done | bytes 114720 | tf_op jit(solution)/shard_map/ppermute | solution.py:565
  23.5 0.9 %outer.1 = f32[8,3,8,128]{3,2,1,0:T(8,128)} custom-call(f32[132,16,128]{2,1,0:T(8,128)S(1)} %inner.1, f32[17,16,128]{2,1,0:T(8,128)S(1)} %middle.1, f32[28,8,128]{2,1,0:T(8,128)S(1)} %collective-permute-done.10.from_below), custom_call_target="tpu_custom_call" | custom-call | tf_op jit(solution)/shard_map/outer/pallas_call | solution.py:526
  (6 shorter events, 0.0 us)
Async XLA Ops:
  0.0 17.1 %copy-start = (s32[3]{0:T(128)S(1)}, s32[3]{0:T(128)}, u32[]{:S(2)}) copy-start(s32[3]{0:T(128)} %row_shift.1) | copy-start | bytes 40
  0.0 9.3 %collective-permute-start.3 = (f32[8,3,8,128]{3,2,1,0:T(8,128)}, f32[8,3,8,128]{3,2,1,0:T(8,128)S(1)}, u32[]{:S(2)}, u32[]{:S(2)}) collective-permute-start(f32[8,3,8,128]{3,2,1,0:T(8,128)} %param.3), channel_id=1, source_target_pairs={{0,2},{1,3},{2,4},{3,5},{4,6},{5,7},{6,0},{7,1},{8,10},{9,11},{10,... | collective-permute-start | bytes 294920 | tf_op jit(solution)/shard_map/ppermute | solution.py:554
  3.0 9.4 %collective-permute-start = (f32[8,3,8,128]{3,2,1,0:T(8,128)}, f32[8,3,8,128]{3,2,1,0:T(8,128)S(1)}, u32[]{:S(2)}, u32[]{:S(2)}) collective-permute-start(f32[8,3,8,128]{3,2,1,0:T(8,128)} %param.3), channel_id=1, source_target_pairs={{0,4},{1,5},{2,6},{3,7},{4,0},{5,1},{6,2},{7,3},{8,12},{9,13},{10,... | collective-permute-start | bytes 294920 | tf_op jit(solution)/shard_map/ppermute | solution.py:554
  5.6 8.1 %collective-permute-start.6 = (f32[8,3,8,128]{3,2,1,0:T(8,128)}, f32[8,3,8,128]{3,2,1,0:T(8,128)S(1)}, u32[]{:S(2)}, u32[]{:S(2)}) collective-permute-start(f32[8,3,8,128]{3,2,1,0:T(8,128)} %param.3), channel_id=1, source_target_pairs={{0,1},{1,0},{2,3},{3,2},{4,5},{5,4},{6,7},{7,6},{8,9},{9,8},{10,11... | collective-permute-start | bytes 294920 | tf_op jit(solution)/shard_map/ppermute | solution.py:542
  5.6 7.4 %collective-permute-start.5 = (f32[8,3,8,128]{3,2,1,0:T(8,128)}, f32[8,3,8,128]{3,2,1,0:T(8,128)S(1)}, u32[]{:S(2)}, u32[]{:S(2)}) collective-permute-start(f32[8,3,8,128]{3,2,1,0:T(8,128)} %param.3), channel_id=1, source_target_pairs={{0,6},{1,7},{2,0},{3,1},{4,2},{5,3},{6,4},{7,5},{8,14},{9,15},{10,... | collective-permute-start | bytes 294920 | tf_op jit(solution)/shard_map/ppermute | solution.py:554
  7.0 3.7 %collective-permute-start.1 = (s32[3]{0:T(128)}, s32[3]{0:T(128)S(1)}, u32[]{:S(2)}, u32[]{:S(2)}) collective-permute-start(s32[3]{0:T(128)} %row_shift.1), channel_id=1, source_target_pairs={{0,8},{1,25},{2,10},{3,27},{4,12},{5,29},{6,14},{7,31},{8,0},{9,17... | collective-permute-start | bytes 44 | tf_op jit(solution)/shard_map/ppermute | solution.py:550
  9.3 3.1 %collective-permute-start.4 = (f32[8,3,8,128]{3,2,1,0:T(8,128)S(1)}, f32[8,3,8,128]{3,2,1,0:T(8,128)S(1)}, u32[]{:S(2)}, u32[]{:S(2)}) collective-permute-start(f32[8,3,8,128]{3,2,1,0:T(8,128)S(1)} %collective-permute-done.3.refs_1_), channel_id=1, source_target_pairs={{0,1},{1,0},{2,3},{3,2},{4,5},{5,4},{6,7},{7,6},{8,9},{9,8},{10,11... | collective-permute-start | bytes 294920 | tf_op jit(solution)/shard_map/ppermute | solution.py:542
  10.6 1.1 %collective-permute-start.2 = (s32[3]{0:T(128)S(1)}, s32[3]{0:T(128)S(1)}, u32[]{:S(2)}, u32[]{:S(2)}) collective-permute-start(s32[3]{0:T(128)S(1)} %collective-permute-done.1.received), channel_id=1, source_target_pairs={{0,1},{1,0},{2,3},{3,2},{4,5},{5,4},{6,7},{7,6},{8,9},{9,8},{10,11... | collective-permute-start | bytes 44 | tf_op jit(solution)/shard_map/ppermute | solution.py:542
  12.4 1.3 %collective-permute-start.7 = (f32[8,3,8,128]{3,2,1,0:T(8,128)S(1)}, f32[8,3,8,128]{3,2,1,0:T(8,128)S(1)}, u32[]{:S(2)}, u32[]{:S(2)}) collective-permute-start(f32[8,3,8,128]{3,2,1,0:T(8,128)S(1)} %collective-permute-done.refs_2_), channel_id=1, source_target_pairs={{0,1},{1,0},{2,3},{3,2},{4,5},{5,4},{6,7},{7,6},{8,9},{9,8},{10,11... | collective-permute-start | bytes 294920 | tf_op jit(solution)/shard_map/ppermute | solution.py:542
  13.0 1.3 %collective-permute-start.8 = (f32[8,3,8,128]{3,2,1,0:T(8,128)S(1)}, f32[8,3,8,128]{3,2,1,0:T(8,128)S(1)}, u32[]{:S(2)}, u32[]{:S(2)}) collective-permute-start(f32[8,3,8,128]{3,2,1,0:T(8,128)S(1)} %collective-permute-done.5.refs_3_), channel_id=1, source_target_pairs={{0,1},{1,0},{2,3},{3,2},{4,5},{5,4},{6,7},{7,6},{8,9},{9,8},{10,11... | collective-permute-start | bytes 294920 | tf_op jit(solution)/shard_map/ppermute | solution.py:542
  14.6 6.3 %collective-permute-start.9 = (f32[31,8,128]{2,1,0:T(8,128)S(1)}, f32[31,8,128]{2,1,0:T(8,128)S(1)}, u32[]{:S(2)}, u32[]{:S(2)}) collective-permute-start(f32[31,8,128]{2,1,0:T(8,128)S(1)} %get-tuple-element.21), channel_id=1, source_target_pairs={{8,0},{16,8},{24,16},{0,24},{9,1},{17,9},{25,17},{1,25},{10,2},{18... | collective-permute-start | bytes 380936 | tf_op jit(solution)/shard_map/ppermute | solution.py:566
  17.1 6.4 %collective-permute-start.10 = (f32[28,8,128]{2,1,0:T(8,128)S(1)}, f32[28,8,128]{2,1,0:T(8,128)S(1)}, u32[]{:S(2)}, u32[]{:S(2)}) collective-permute-start(f32[28,8,128]{2,1,0:T(8,128)S(1)} %get-tuple-element.22), channel_id=1, source_target_pairs={{0,8},{8,16},{16,24},{24,0},{1,9},{9,17},{17,25},{25,1},{2,10},{10... | collective-permute-start | bytes 344072 | tf_op jit(solution)/shard_map/ppermute | solution.py:565

commit v4 on v3

--- a/solution.py
+++ b/solution.py
@@ -304,7 +304,7 @@
         known[key[0]][key[1:]] = jnp.concatenate([main, edges.get(key, main)], axis=0)
 
 
-def windows_call(near, far, received, swapped, offset):
+def windows_down_call(near, far, received, swapped, offset):
     count = len(near)
     parts, cells_x, cells_y, cells_z = near[0].shape
     blocks = 2 * count
@@ -338,8 +338,7 @@
                     whole[place] = block[...]
         sub = lax.broadcasted_iota(jnp.int32, (cells_y, cells_z), 0)
         for out, shift_by, wanted, end, sign, turn in (
-            (outs[0], above, lows, last, 1, cells_x),
-            (outs[1], below, highs, 0, -1, -cells_x),
+            (outs[0], below, highs, 0, -1, -cells_x),
         ):
             at_end = place_x == end
             away = jnp.where(at_end, sign * offset[0], 0)
@@ -364,13 +363,67 @@
         out_shape=[jax.ShapeDtypeStruct((blocks, parts, cells_x, cells_y, cells_z), jnp.float32)]
         + [
             jax.ShapeDtypeStruct((message_tiles(wanted), cells_y, cells_z), jnp.float32)
-            for wanted in (lows, highs)
+            for wanted in (highs,)
         ],
         in_specs=[smem] + [vmem] * (2 + blocks),
-        out_specs=[vmem] * 3,
+        out_specs=[vmem] * 2,
+        cost_estimate=pl.CostEstimate(flops=1, bytes_accessed=1, transcendentals=0),
         compiler_params=pltpu.CompilerParams(vmem_limit_bytes=32 * 1024 * 1024),
-        name="windows",
+        name="windows_down",
     )(offset, received, swapped, *near, *far)
+
+
+def windows_up_call(whole, received, swapped, offset):
+    blocks, parts, cells_x, cells_y, cells_z = whole.shape
+    length = blocks * cells_y
+    lows, highs = low_windows(cells_x), high_windows(cells_x)
+
+    def body(offset, received, swapped, whole, *outs):
+        place_x, place_y = lax.axis_index("gx"), lax.axis_index("gy")
+        here = remainder(place_x + place_y, 2) == 0
+        lane = lax.broadcasted_iota(jnp.int32, (1, cells_x), 1)
+        one, other = (
+            source[...].reshape(1, cells_x).astype(jnp.float32) for source in (received, swapped)
+        )
+
+        def scalars(values):
+            return [
+                jnp.sum(jnp.where(lane == i, values, 0.0)).astype(jnp.int32) for i in range(cells_x)
+            ]
+
+        above, below = scalars(jnp.where(here, one, other)), scalars(jnp.where(here, other, one))
+        last = lax.axis_size("gx") - 1
+        sub = lax.broadcasted_iota(jnp.int32, (cells_y, cells_z), 0)
+        for out, shift_by, wanted, end, sign, turn in (
+            (outs[0], above, lows, last, 1, cells_x),
+        ):
+            at_end = place_x == end
+            away = jnp.where(at_end, sign * offset[0], 0)
+            boost = jnp.where(at_end, sign * shear_speed, 0.0)
+            known = {}
+            for row, radial in wanted:
+                start = remainder(place_y * cells_y - shift_by[row] + away + 2 * length, length)
+                read = tile_reader(whole, start, length, -1, 3)
+                raw = []
+                for component in range(parts):
+                    before, main, after = read(component, radial + turn)
+                    raw.append(jnp.concatenate([main, jnp.where(sub < 4, after, before)], axis=0))
+                raw[2] = raw[2] + boost * raw[0]
+                for component in range(parts):
+                    known.setdefault(row, {})["raw", radial - row + 2, component] = raw[component]
+            pack(out, wanted, {row: Row(found) for row, found in known.items()})
+
+    vmem = pl.BlockSpec(memory_space=pltpu.VMEM)
+    smem = pl.BlockSpec(memory_space=pltpu.SMEM)
+    return pl.pallas_call(
+        body,
+        out_shape=jax.ShapeDtypeStruct((message_tiles(lows), cells_y, cells_z), jnp.float32),
+        in_specs=[smem] + [vmem] * 3,
+        out_specs=vmem,
+        cost_estimate=pl.CostEstimate(flops=1, bytes_accessed=1, transcendentals=0),
+        compiler_params=pltpu.CompilerParams(vmem_limit_bytes=32 * 1024 * 1024),
+        name="windows_up",
+    )(offset, received, swapped, whole)
 
 
 def reads(key):
@@ -503,7 +556,7 @@
         in_specs=[vmem] * 2,
         out_specs=vmem,
         compiler_params=pltpu.CompilerParams(vmem_limit_bytes=32 * 1024 * 1024),
-        cost_estimate=pl.CostEstimate(flops=10**6, bytes_accessed=10**6, transcendentals=10**4),
+        cost_estimate=pl.CostEstimate(flops=10**9, bytes_accessed=10**7, transcendentals=0),
         name="middle",
     )(inner, from_above)
 
@@ -561,9 +614,10 @@
     passed_on[3], _ = lax.optimization_barrier((near[3], passed_on[2]))
     far += [other_core(values) for values in passed_on[3:]]
     near[0] = own
-    whole, to_above, to_below = windows_call(near, far, received, swapped, shear_offset)
+    whole, to_below = windows_down_call(near, far, received, swapped, shear_offset)
+    from_above = lax.ppermute(to_below, "gx", downward)
+    to_above = windows_up_call(whole, received, swapped, shear_offset)
     from_below = lax.ppermute(to_above, "gx", upward)
-    from_above = lax.ppermute(to_below, "gx", downward)
     inner = inner_call(whole, row_shift)
     middle = middle_call(inner, from_above, fields.shape[1])
     return outer_call(inner, middle, from_below, fields.shape[1], fields.shape[0])

time: 24.6 us -> 24.6 us (level)
  waiting for transfers between devices: 7.67 us -> 7.4 us
    ppermute x1, waiting for transfers between devices: 2.47 us -> 2.2 us  [on_device(): from_above = lax.ppermute(to_below, 'gx', downward)]
  transfers between devices with their start and end apart: 11 -> 11, of which waited for: 7 -> 7; matrix products, arithmetic and copies ran while one was open for 3% -> 3% of each run, Pallas kernels for 8% -> 9%
where the time goes in v4:
time: 24.6 us; the launch traced here: 24.5 us
  starting transfers between devices  12.2 us (50%)
  waiting for transfers between devices  7.4 us (30%)
  Pallas kernels  3.29 us (13%)
  local copies, waits for them, and re-layouts  0.83 us (3%)
  between operations  0.7 us (3%)
    ppermute x3, starting transfers between devices, on_device(): lax.ppermute(fields, 'gy', [(i, (i + step) % count_y) for i in range(coun...  6.96 us
    ppermute x1, starting transfers between devices, on_device(): from_above = lax.ppermute(to_below, 'gx', downward)  2.49 us
    ppermute x1, waiting for transfers between devices, on_device(): from_above = lax.ppermute(to_below, 'gx', downward)  2.2 us
    ppermute x1, waiting for transfers between devices, on_device(): from_below = lax.ppermute(to_above, 'gx', upward)  2.07 us
    ppermute x1, starting transfers between devices, on_device(): received = lax.ppermute(row_shift, ('gx', 'gy'), meet)  1.49 us
    ppermute x5, waiting for transfers between devices, other_core(): return lax.ppermute(values, 'gy', [(i, i ^ 1) for i in range(count_y)])  1.48 us
    pallas_call x1, Pallas kernels, inner_call(): pl.pallas_call(body, out_shape=jax.ShapeDtypeStruct((total, 2 * cells_y,...  1.29 us
    ppermute x3, waiting for transfers between devices, on_device(): lax.ppermute(fields, 'gy', [(i, (i + step) % count_y) for i in range(coun...  1.28 us
  transfers between devices with their start and end apart: 11, of which 7 were waited for; matrix products, arithmetic and copies ran while one was open for 3% of the time, Pallas kernels for 9%

profile of v4, /device:TPU:0, one launch (start us, length us, event | category | flops | bytes accessed | tf_op | source)
XLA Modules:
  0.0 24.5 jit_solution(3466315992549084019)
XLA Ops:
  0.0 3.0 %collective-permute-start.3 = (f32[8,3,8,128]{3,2,1,0:T(8,128)}, f32[8,3,8,128]{3,2,1,0:T(8,128)S(1)}, u32[]{:S(2)}, u32[]{:S(2)}) collective-permute-start(f32[8,3,8,128]{3,2,1,0:T(8,128)} %param.3), channel_id=1, source_target_pairs={{0,2},{1,3},{2,4},{3,5},{4,6},{5,7},{6,0},{7,1},{8,10},{9,11},{10,... | collective-permute-start | bytes 294920 | tf_op jit(solution)/shard_map/ppermute | solution.py:607
  3.0 2.6 %collective-permute-start = (f32[8,3,8,128]{3,2,1,0:T(8,128)}, f32[8,3,8,128]{3,2,1,0:T(8,128)S(1)}, u32[]{:S(2)}, u32[]{:S(2)}) collective-permute-start(f32[8,3,8,128]{3,2,1,0:T(8,128)} %param.3), channel_id=1, source_target_pairs={{0,4},{1,5},{2,6},{3,7},{4,0},{5,1},{6,2},{7,3},{8,12},{9,13},{10,... | collective-permute-start | bytes 294920 | tf_op jit(solution)/shard_map/ppermute | solution.py:607
  5.6 1.3 %collective-permute-start.5 = (f32[8,3,8,128]{3,2,1,0:T(8,128)}, f32[8,3,8,128]{3,2,1,0:T(8,128)S(1)}, u32[]{:S(2)}, u32[]{:S(2)}) collective-permute-start(f32[8,3,8,128]{3,2,1,0:T(8,128)} %param.3), channel_id=1, source_target_pairs={{0,6},{1,7},{2,0},{3,1},{4,2},{5,3},{6,4},{7,5},{8,14},{9,15},{10,... | collective-permute-start | bytes 294920 | tf_op jit(solution)/shard_map/ppermute | solution.py:607
  7.0 1.5 %collective-permute-start.1 = (s32[3]{0:T(128)}, s32[3]{0:T(128)S(1)}, u32[]{:S(2)}, u32[]{:S(2)}) collective-permute-start(s32[3]{0:T(128)} %row_shift.1), channel_id=1, source_target_pairs={{0,8},{1,25},{2,10},{3,27},{4,12},{5,29},{6,14},{7,31},{8,0},{9,17... | collective-permute-start | bytes 44 | tf_op jit(solution)/shard_map/ppermute | solution.py:603
  8.5 0.8 %fusion = (f32[4,3,8,128]{3,2,1,0:T(8,128)S(1)}, f32[4,3,8,128]{3,2,1,0:T(8,128)S(1)}) fusion(f32[8,3,8,128]{3,2,1,0:T(8,128)} %param.3), kind=kLoop, calls=%fused_computation.1 | loop fusion | bytes 196608 | tf_op jit(solution)/shard_map/jit(_roll_static)/slice | solution.py:597
  9.3 0.0 collective-permute-done.3.refs_1_
  9.3 1.0 %collective-permute-start.4 = (f32[8,3,8,128]{3,2,1,0:T(8,128)S(1)}, f32[8,3,8,128]{3,2,1,0:T(8,128)S(1)}, u32[]{:S(2)}, u32[]{:S(2)}) collective-permute-start(f32[8,3,8,128]{3,2,1,0:T(8,128)S(1)} %collective-permute-done.3.refs_1_), channel_id=1, source_target_pairs={{0,1},{1,0},{2,3},{3,2},{4,5},{5,4},{6,7},{7,6},{8,9},{9,8},{10,11... | collective-permute-start | bytes 294920 | tf_op jit(solution)/shard_map/ppermute | solution.py:595
  10.3 0.4 %collective-permute-done.1.received = s32[3]{0:T(128)S(1)} collective-permute-done((s32[3]{0:T(128)}, s32[3]{0:T(128)S(1)}, u32[]{:S(2)}, u32[]{:S(2)}) %collective-permute-start.1) | collective-permute-done | bytes 44 | tf_op jit(solution)/shard_map/ppermute | solution.py:603
  10.6 0.3 %collective-permute-start.2 = (s32[3]{0:T(128)S(1)}, s32[3]{0:T(128)S(1)}, u32[]{:S(2)}, u32[]{:S(2)}) collective-permute-start(s32[3]{0:T(128)S(1)} %collective-permute-done.1.received), channel_id=1, source_target_pairs={{0,1},{1,0},{2,3},{3,2},{4,5},{5,4},{6,7},{7,6},{8,9},{9,8},{10,11... | collective-permute-start | bytes 44 | tf_op jit(solution)/shard_map/ppermute | solution.py:595
  10.9 0.8 %collective-permute-done.2.swapped = s32[3]{0:T(128)S(1)} collective-permute-done((s32[3]{0:T(128)S(1)}, s32[3]{0:T(128)S(1)}, u32[]{:S(2)}, u32[]{:S(2)}) %collective-permute-start.2) | collective-permute-done | bytes 44 | tf_op jit(solution)/shard_map/ppermute | solution.py:595
  11.8 0.6 %collective-permute-done.refs_2_ = f32[8,3,8,128]{3,2,1,0:T(8,128)S(1)} collective-permute-done((f32[8,3,8,128]{3,2,1,0:T(8,128)}, f32[8,3,8,128]{3,2,1,0:T(8,128)S(1)}, u32[]{:S(2)}, u32[]{:S(2)}) %collective-permute-start) | collective-permute-done | bytes 98336 | tf_op jit(solution)/shard_map/ppermute | solution.py:607
  12.4 0.6 %collective-permute-done.5.refs_3_ = f32[8,3,8,128]{3,2,1,0:T(8,128)S(1)} collective-permute-done((f32[8,3,8,128]{3,2,1,0:T(8,128)}, f32[8,3,8,128]{3,2,1,0:T(8,128)S(1)}, u32[]{:S(2)}, u32[]{:S(2)}) %collective-permute-start.5) | collective-permute-done | bytes 98336 | tf_op jit(solution)/shard_map/ppermute | solution.py:607
  13.7 0.0 collective-permute-done.6.refs_4_
  13.7 0.0 collective-permute-done.7.refs_6_
  13.7 0.6 %collective-permute-done.8.refs_7_ = f32[8,3,8,128]{3,2,1,0:T(8,128)S(1)} collective-permute-done((f32[8,3,8,128]{3,2,1,0:T(8,128)S(1)}, f32[8,3,8,128]{3,2,1,0:T(8,128)S(1)}, u32[]{:S(2)}, u32[]{:S(2)}) %collective-permute-start.8) | collective-permute-done | bytes 98336 | tf_op jit(solution)/shard_map/ppermute | solution.py:595
  14.3 0.2 %windows_down.1 = (f32[8,8,3,8,128]{4,3,2,1,0:T(8,128)S(1)}, f32[31,8,128]{2,1,0:T(8,128)S(1)}) custom-call(s32[1]{0:T(128)S(6)} %copy.4.offset, s32[3]{0:T(128)S(1)} %collective-permute-done.1.received, s32[3]{0:T(128)S(1)} %collective-permute-done.2.swapped, f32[8,3,8,128]{3,2,1,0:T(8,128)S(1)} %pad_maximum_fusion.refs_0_, ...), custom_call_target="tpu_custom_call" | custom-call | flops 1 | bytes 1 | tf_op jit(solution)/shard_map/windows_down/pallas_call | solution.py:361
  14.6 2.5 %collective-permute-start.9 = (f32[31,8,128]{2,1,0:T(8,128)S(1)}, f32[31,8,128]{2,1,0:T(8,128)S(1)}, u32[]{:S(2)}, u32[]{:S(2)}) collective-permute-start(f32[31,8,128]{2,1,0:T(8,128)S(1)} %get-tuple-element.20), channel_id=1, source_target_pairs={{8,0},{16,8},{24,16},{0,24},{9,1},{17,9},{25,17},{1,25},{10,2},{18... | collective-permute-start | bytes 380936 | tf_op jit(solution)/shard_map/ppermute | solution.py:618
  17.1 0.2 windows_up.1
  17.3 0.0 collective-permute-start.10
  17.4 1.3 %inner.1 = f32[132,16,128]{2,1,0:T(8,128)S(1)} custom-call(s32[3]{0:T(128)S(1)} %copy-done, f32[8,8,3,8,128]{4,3,2,1,0:T(8,128)S(1)} %get-tuple-element.19.whole), custom_call_target="tpu_custom_call" | custom-call | flops 10000000 | bytes 1000000 | tf_op jit(solution)/shard_map/inner/pallas_call | solution.py:518
  18.6 2.2 %collective-permute-done.9.from_above = f32[31,8,128]{2,1,0:T(8,128)S(1)} collective-permute-done((f32[31,8,128]{2,1,0:T(8,128)S(1)}, f32[31,8,128]{2,1,0:T(8,128)S(1)}, u32[]{:S(2)}, u32[]{:S(2)}) %collective-permute-start.9) | collective-permute-done | bytes 127008 | tf_op jit(solution)/shard_map/ppermute | solution.py:618
  20.9 0.6 %middle.1 = f32[17,16,128]{2,1,0:T(8,128)S(1)} custom-call(f32[132,16,128]{2,1,0:T(8,128)S(1)} %inner.1, f32[31,8,128]{2,1,0:T(8,128)S(1)} %collective-permute-done.9.from_above), custom_call_target="tpu_custom_call" | custom-call | flops 1000000000 | bytes 10000000 | tf_op jit(solution)/shard_map/middle/pallas_call | solution.py:553
  21.4 2.1 %collective-permute-done.10.from_below = f32[28,8,128]{2,1,0:T(8,128)S(1)} collective-permute-done((f32[28,8,128]{2,1,0:T(8,128)S(1)}, f32[28,8,128]{2,1,0:T(8,128)S(1)}, u32[]{:S(2)}, u32[]{:S(2)}) %collective-permute-start.10) | collective-permute-done | bytes 114720 | tf_op jit(solution)/shard_map/ppermute | solution.py:620
  23.5 0.9 %outer.1 = f32[8,3,8,128]{3,2,1,0:T(8,128)} custom-call(f32[132,16,128]{2,1,0:T(8,128)S(1)} %inner.1, f32[17,16,128]{2,1,0:T(8,128)S(1)} %middle.1, f32[28,8,128]{2,1,0:T(8,128)S(1)} %collective-permute-done.10.from_below), custom_call_target="tpu_custom_call" | custom-call | tf_op jit(solution)/shard_map/outer/pallas_call | solution.py:579
  (7 shorter events, 0.0 us)
Async XLA Ops:
  0.0 17.3 %copy-start = (s32[3]{0:T(128)S(1)}, s32[3]{0:T(128)}, u32[]{:S(2)}) copy-start(s32[3]{0:T(128)} %row_shift.1) | copy-start | bytes 40
  0.0 9.3 %collective-permute-start.3 = (f32[8,3,8,128]{3,2,1,0:T(8,128)}, f32[8,3,8,128]{3,2,1,0:T(8,128)S(1)}, u32[]{:S(2)}, u32[]{:S(2)}) collective-permute-start(f32[8,3,8,128]{3,2,1,0:T(8,128)} %param.3), channel_id=1, source_target_pairs={{0,2},{1,3},{2,4},{3,5},{4,6},{5,7},{6,0},{7,1},{8,10},{9,11},{10,... | collective-permute-start | bytes 294920 | tf_op jit(solution)/shard_map/ppermute | solution.py:607
  3.0 9.4 %collective-permute-start = (f32[8,3,8,128]{3,2,1,0:T(8,128)}, f32[8,3,8,128]{3,2,1,0:T(8,128)S(1)}, u32[]{:S(2)}, u32[]{:S(2)}) collective-permute-start(f32[8,3,8,128]{3,2,1,0:T(8,128)} %param.3), channel_id=1, source_target_pairs={{0,4},{1,5},{2,6},{3,7},{4,0},{5,1},{6,2},{7,3},{8,12},{9,13},{10,... | collective-permute-start | bytes 294920 | tf_op jit(solution)/shard_map/ppermute | solution.py:607
  5.6 8.1 %collective-permute-start.6 = (f32[8,3,8,128]{3,2,1,0:T(8,128)}, f32[8,3,8,128]{3,2,1,0:T(8,128)S(1)}, u32[]{:S(2)}, u32[]{:S(2)}) collective-permute-start(f32[8,3,8,128]{3,2,1,0:T(8,128)} %param.3), channel_id=1, source_target_pairs={{0,1},{1,0},{2,3},{3,2},{4,5},{5,4},{6,7},{7,6},{8,9},{9,8},{10,11... | collective-permute-start | bytes 294920 | tf_op jit(solution)/shard_map/ppermute | solution.py:595
  5.6 7.4 %collective-permute-start.5 = (f32[8,3,8,128]{3,2,1,0:T(8,128)}, f32[8,3,8,128]{3,2,1,0:T(8,128)S(1)}, u32[]{:S(2)}, u32[]{:S(2)}) collective-permute-start(f32[8,3,8,128]{3,2,1,0:T(8,128)} %param.3), channel_id=1, source_target_pairs={{0,6},{1,7},{2,0},{3,1},{4,2},{5,3},{6,4},{7,5},{8,14},{9,15},{10,... | collective-permute-start | bytes 294920 | tf_op jit(solution)/shard_map/ppermute | solution.py:607
  7.0 3.7 %collective-permute-start.1 = (s32[3]{0:T(128)}, s32[3]{0:T(128)S(1)}, u32[]{:S(2)}, u32[]{:S(2)}) collective-permute-start(s32[3]{0:T(128)} %row_shift.1), channel_id=1, source_target_pairs={{0,8},{1,25},{2,10},{3,27},{4,12},{5,29},{6,14},{7,31},{8,0},{9,17... | collective-permute-start | bytes 44 | tf_op jit(solution)/shard_map/ppermute | solution.py:603
  9.3 3.1 %collective-permute-start.4 = (f32[8,3,8,128]{3,2,1,0:T(8,128)S(1)}, f32[8,3,8,128]{3,2,1,0:T(8,128)S(1)}, u32[]{:S(2)}, u32[]{:S(2)}) collective-permute-start(f32[8,3,8,128]{3,2,1,0:T(8,128)S(1)} %collective-permute-done.3.refs_1_), channel_id=1, source_target_pairs={{0,1},{1,0},{2,3},{3,2},{4,5},{5,4},{6,7},{7,6},{8,9},{9,8},{10,11... | collective-permute-start | bytes 294920 | tf_op jit(solution)/shard_map/ppermute | solution.py:595
  10.6 1.1 %collective-permute-start.2 = (s32[3]{0:T(128)S(1)}, s32[3]{0:T(128)S(1)}, u32[]{:S(2)}, u32[]{:S(2)}) collective-permute-start(s32[3]{0:T(128)S(1)} %collective-permute-done.1.received), channel_id=1, source_target_pairs={{0,1},{1,0},{2,3},{3,2},{4,5},{5,4},{6,7},{7,6},{8,9},{9,8},{10,11... | collective-permute-start | bytes 44 | tf_op jit(solution)/shard_map/ppermute | solution.py:595
  12.4 1.3 %collective-permute-start.7 = (f32[8,3,8,128]{3,2,1,0:T(8,128)S(1)}, f32[8,3,8,128]{3,2,1,0:T(8,128)S(1)}, u32[]{:S(2)}, u32[]{:S(2)}) collective-permute-start(f32[8,3,8,128]{3,2,1,0:T(8,128)S(1)} %collective-permute-done.refs_2_), channel_id=1, source_target_pairs={{0,1},{1,0},{2,3},{3,2},{4,5},{5,4},{6,7},{7,6},{8,9},{9,8},{10,11... | collective-permute-start | bytes 294920 | tf_op jit(solution)/shard_map/ppermute | solution.py:595
  13.0 1.3 %collective-permute-start.8 = (f32[8,3,8,128]{3,2,1,0:T(8,128)S(1)}, f32[8,3,8,128]{3,2,1,0:T(8,128)S(1)}, u32[]{:S(2)}, u32[]{:S(2)}) collective-permute-start(f32[8,3,8,128]{3,2,1,0:T(8,128)S(1)} %collective-permute-done.5.refs_3_), channel_id=1, source_target_pairs={{0,1},{1,0},{2,3},{3,2},{4,5},{5,4},{6,7},{7,6},{8,9},{9,8},{10,11... | collective-permute-start | bytes 294920 | tf_op jit(solution)/shard_map/ppermute | solution.py:595
  14.6 6.3 %collective-permute-start.9 = (f32[31,8,128]{2,1,0:T(8,128)S(1)}, f32[31,8,128]{2,1,0:T(8,128)S(1)}, u32[]{:S(2)}, u32[]{:S(2)}) collective-permute-start(f32[31,8,128]{2,1,0:T(8,128)S(1)} %get-tuple-element.20), channel_id=1, source_target_pairs={{8,0},{16,8},{24,16},{0,24},{9,1},{17,9},{25,17},{1,25},{10,2},{18... | collective-permute-start | bytes 380936 | tf_op jit(solution)/shard_map/ppermute | solution.py:618
  17.3 6.2 %collective-permute-start.10 = (f32[28,8,128]{2,1,0:T(8,128)S(1)}, f32[28,8,128]{2,1,0:T(8,128)S(1)}, u32[]{:S(2)}, u32[]{:S(2)}) collective-permute-start(f32[28,8,128]{2,1,0:T(8,128)S(1)} %windows_up.1), channel_id=1, source_target_pairs={{0,8},{8,16},{16,24},{24,0},{1,9},{9,17},{17,25},{25,1},{2,10},{10... | collective-permute-start | bytes 344072 | tf_op jit(solution)/shard_map/ppermute | solution.py:620

commit v5 on v3

--- a/solution.py
+++ b/solution.py
@@ -555,7 +555,8 @@
         for step in range(2, count_y, 2)
     ]
     passed_on = list(near)
-    far = [other_core(near[0]), other_core(near[1])]
+    late, _ = lax.optimization_barrier((near[0], near[1]))
+    far = [other_core(late), other_core(near[1])]
     passed_on[2], received, swapped, _ = lax.optimization_barrier((near[2], received, swapped, far[1]))
     far.append(other_core(passed_on[2]))
     passed_on[3], _ = lax.optimization_barrier((near[3], passed_on[2]))

time: 24.6 us -> 24.4 us (level)
    ppermute x1, waiting for transfers between devices: 0.37 us -> 1.25 us  [on_device(): received = lax.ppermute(row_shift, ('gx', 'gy'), meet)]
    ppermute x3, waiting for transfers between devices: 1.28 us -> 0.68 us  [on_device(): lax.ppermute(fields, 'gy', [(i, (i + step) % count_y) for i in range(coun...]
    ppermute x5, waiting for transfers between devices: 1.48 us -> 0.9 us  [other_core(): return lax.ppermute(values, 'gy', [(i, i ^ 1) for i in range(count_y)])]
where the time goes in v5:
time: 24.4 us; the launch traced here: 24.2 us
  starting transfers between devices  12 us (49%)
  waiting for transfers between devices  7.56 us (31%)
  Pallas kernels  3.08 us (13%)
  local copies, waits for them, and re-layouts  0.83 us (3%)
  between operations  0.7 us (3%)
    ppermute x3, starting transfers between devices, on_device(): lax.ppermute(fields, 'gy', [(i, (i + step) % count_y) for i in range(coun...  6.96 us
    ppermute x1, starting transfers between devices, on_device(): from_above = lax.ppermute(to_below, 'gx', downward)  2.51 us
    ppermute x1, waiting for transfers between devices, on_device(): from_above = lax.ppermute(to_below, 'gx', downward)  2.48 us
    ppermute x1, waiting for transfers between devices, on_device(): from_below = lax.ppermute(to_above, 'gx', upward)  2.25 us
    ppermute x1, starting transfers between devices, on_device(): received = lax.ppermute(row_shift, ('gx', 'gy'), meet)  1.49 us
    pallas_call x1, Pallas kernels, inner_call(): pl.pallas_call(body, out_shape=jax.ShapeDtypeStruct((total, 2 * cells_y,...  1.29 us
    ppermute x1, waiting for transfers between devices, on_device(): received = lax.ppermute(row_shift, ('gx', 'gy'), meet)  1.25 us
    ppermute x5, starting transfers between devices, other_core(): return lax.ppermute(values, 'gy', [(i, i ^ 1) for i in range(count_y)])  1.06 us
  transfers between devices with their start and end apart: 11, of which 7 were waited for; matrix products, arithmetic and copies ran while one was open for 3% of the time, Pallas kernels for 8%

profile of v5, /device:TPU:0, one launch (start us, length us, event | category | flops | bytes accessed | tf_op | source)
XLA Modules:
  0.0 24.2 jit_solution(8154509573010101944)
XLA Ops:
  0.0 3.0 %collective-permute-start.3 = (f32[8,3,8,128]{3,2,1,0:T(8,128)}, f32[8,3,8,128]{3,2,1,0:T(8,128)S(1)}, u32[]{:S(2)}, u32[]{:S(2)}) collective-permute-start(f32[8,3,8,128]{3,2,1,0:T(8,128)} %param.3), channel_id=1, source_target_pairs={{0,2},{1,3},{2,4},{3,5},{4,6},{5,7},{6,0},{7,1},{8,10},{9,11},{10,... | collective-permute-start | bytes 294920 | tf_op jit(solution)/shard_map/ppermute | solution.py:554
  3.0 2.6 %collective-permute-start = (f32[8,3,8,128]{3,2,1,0:T(8,128)}, f32[8,3,8,128]{3,2,1,0:T(8,128)S(1)}, u32[]{:S(2)}, u32[]{:S(2)}) collective-permute-start(f32[8,3,8,128]{3,2,1,0:T(8,128)} %param.3), channel_id=1, source_target_pairs={{0,4},{1,5},{2,6},{3,7},{4,0},{5,1},{6,2},{7,3},{8,12},{9,13},{10,... | collective-permute-start | bytes 294920 | tf_op jit(solution)/shard_map/ppermute | solution.py:554
  5.6 1.3 %collective-permute-start.5 = (f32[8,3,8,128]{3,2,1,0:T(8,128)}, f32[8,3,8,128]{3,2,1,0:T(8,128)S(1)}, u32[]{:S(2)}, u32[]{:S(2)}) collective-permute-start(f32[8,3,8,128]{3,2,1,0:T(8,128)} %param.3), channel_id=1, source_target_pairs={{0,6},{1,7},{2,0},{3,1},{4,2},{5,3},{6,4},{7,5},{8,14},{9,15},{10,... | collective-permute-start | bytes 294920 | tf_op jit(solution)/shard_map/ppermute | solution.py:554
  7.0 1.5 %collective-permute-start.1 = (s32[3]{0:T(128)}, s32[3]{0:T(128)S(1)}, u32[]{:S(2)}, u32[]{:S(2)}) collective-permute-start(s32[3]{0:T(128)} %row_shift.1), channel_id=1, source_target_pairs={{0,8},{1,25},{2,10},{3,27},{4,12},{5,29},{6,14},{7,31},{8,0},{9,17... | collective-permute-start | bytes 44 | tf_op jit(solution)/shard_map/ppermute | solution.py:550
  8.5 0.8 %fusion = (f32[4,3,8,128]{3,2,1,0:T(8,128)S(1)}, f32[4,3,8,128]{3,2,1,0:T(8,128)S(1)}) fusion(f32[8,3,8,128]{3,2,1,0:T(8,128)} %param.3), kind=kLoop, calls=%fused_computation.1 | loop fusion | bytes 196608 | tf_op jit(solution)/shard_map/jit(_roll_static)/slice | solution.py:544
  9.3 0.0 collective-permute-done.3.refs_1_
  9.3 0.1 collective-permute-start.4
  9.4 1.3 %collective-permute-done.1.received = s32[3]{0:T(128)S(1)} collective-permute-done((s32[3]{0:T(128)}, s32[3]{0:T(128)S(1)}, u32[]{:S(2)}, u32[]{:S(2)}) %collective-permute-start.1) | collective-permute-done | bytes 44 | tf_op jit(solution)/shard_map/ppermute | solution.py:550
  10.6 0.5 %collective-permute-start.6 = (f32[8,3,8,128]{3,2,1,0:T(8,128)}, f32[8,3,8,128]{3,2,1,0:T(8,128)S(1)}, u32[]{:S(2)}, u32[]{:S(2)}) collective-permute-start(f32[8,3,8,128]{3,2,1,0:T(8,128)} %param.3), channel_id=1, source_target_pairs={{0,1},{1,0},{2,3},{3,2},{4,5},{5,4},{6,7},{7,6},{8,9},{9,8},{10,11... | collective-permute-start | bytes 294920 | tf_op jit(solution)/shard_map/ppermute | solution.py:542
  11.2 0.6 %collective-permute-done.2.swapped = s32[3]{0:T(128)S(1)} collective-permute-done((s32[3]{0:T(128)S(1)}, s32[3]{0:T(128)S(1)}, u32[]{:S(2)}, u32[]{:S(2)}) %collective-permute-start.2) | collective-permute-done | bytes 44 | tf_op jit(solution)/shard_map/ppermute | solution.py:542
  11.8 0.6 %collective-permute-done.refs_2_ = f32[8,3,8,128]{3,2,1,0:T(8,128)S(1)} collective-permute-done((f32[8,3,8,128]{3,2,1,0:T(8,128)}, f32[8,3,8,128]{3,2,1,0:T(8,128)S(1)}, u32[]{:S(2)}, u32[]{:S(2)}) %collective-permute-start) | collective-permute-done | bytes 98336 | tf_op jit(solution)/shard_map/ppermute | solution.py:554
  12.4 0.0 collective-permute-done.4.refs_5_
  12.4 0.0 collective-permute-start.7
  12.4 0.0 collective-permute-done.5.refs_3_
  12.5 0.5 %collective-permute-start.8 = (f32[8,3,8,128]{3,2,1,0:T(8,128)S(1)}, f32[8,3,8,128]{3,2,1,0:T(8,128)S(1)}, u32[]{:S(2)}, u32[]{:S(2)}) collective-permute-start(f32[8,3,8,128]{3,2,1,0:T(8,128)S(1)} %collective-permute-done.5.refs_3_), channel_id=1, source_target_pairs={{0,1},{1,0},{2,3},{3,2},{4,5},{5,4},{6,7},{7,6},{8,9},{9,8},{10,11... | collective-permute-start | bytes 294920 | tf_op jit(solution)/shard_map/ppermute | solution.py:542
  13.6 0.1 collective-permute-done.7.refs_6_
  13.7 0.2 collective-permute-done.8.refs_7_
  13.9 0.3 %windows.1 = (f32[8,8,3,8,128]{4,3,2,1,0:T(8,128)S(1)}, f32[28,8,128]{2,1,0:T(8,128)S(1)}, f32[31,8,128]{2,1,0:T(8,128)S(1)}) custom-call(s32[1]{0:T(128)S(6)} %copy.4.offset, s32[3]{0:T(128)S(1)} %collective-permute-done.1.received, s32[3]{0:T(128)S(1)} %collective-permute-done.2.swapped, f32[8,3,8,128]{3,2,1,0:T(8,128)S(1)} %pad_maximum_fusion.refs_0_, ...), custom_call_target="tpu_custom_call" | custom-call | tf_op jit(solution)/shard_map/windows/pallas_call | solution.py:362
  14.1 2.5 %collective-permute-start.9 = (f32[31,8,128]{2,1,0:T(8,128)S(1)}, f32[31,8,128]{2,1,0:T(8,128)S(1)}, u32[]{:S(2)}, u32[]{:S(2)}) collective-permute-start(f32[31,8,128]{2,1,0:T(8,128)S(1)} %get-tuple-element.23), channel_id=1, source_target_pairs={{8,0},{16,8},{24,16},{0,24},{9,1},{17,9},{25,17},{1,25},{10,2},{18... | collective-permute-start | bytes 380936 | tf_op jit(solution)/shard_map/ppermute | solution.py:567
  16.6 1.3 %inner.1 = f32[132,16,128]{2,1,0:T(8,128)S(1)} custom-call(s32[3]{0:T(128)S(1)} %copy-done, f32[8,8,3,8,128]{4,3,2,1,0:T(8,128)S(1)} %get-tuple-element.22.whole), custom_call_target="tpu_custom_call" | custom-call | flops 10000000 | bytes 1000000 | tf_op jit(solution)/shard_map/inner/pallas_call | solution.py:465
  17.9 2.5 %collective-permute-done.9.from_above = f32[31,8,128]{2,1,0:T(8,128)S(1)} collective-permute-done((f32[31,8,128]{2,1,0:T(8,128)S(1)}, f32[31,8,128]{2,1,0:T(8,128)S(1)}, u32[]{:S(2)}, u32[]{:S(2)}) %collective-permute-start.9) | collective-permute-done | bytes 127008 | tf_op jit(solution)/shard_map/ppermute | solution.py:567
  20.4 0.6 %middle.1 = f32[17,16,128]{2,1,0:T(8,128)S(1)} custom-call(f32[132,16,128]{2,1,0:T(8,128)S(1)} %inner.1, f32[31,8,128]{2,1,0:T(8,128)S(1)} %collective-permute-done.9.from_above), custom_call_target="tpu_custom_call" | custom-call | flops 1000000 | bytes 1000000 | tf_op jit(solution)/shard_map/middle/pallas_call | solution.py:500
  21.0 2.2 %collective-permute-done.10.from_below = f32[28,8,128]{2,1,0:T(8,128)S(1)} collective-permute-done((f32[28,8,128]{2,1,0:T(8,128)S(1)}, f32[28,8,128]{2,1,0:T(8,128)S(1)}, u32[]{:S(2)}, u32[]{:S(2)}) %collective-permute-start.10) | collective-permute-done | bytes 114720 | tf_op jit(solution)/shard_map/ppermute | solution.py:566
  23.3 0.9 %outer.1 = f32[8,3,8,128]{3,2,1,0:T(8,128)} custom-call(f32[132,16,128]{2,1,0:T(8,128)S(1)} %inner.1, f32[17,16,128]{2,1,0:T(8,128)S(1)} %middle.1, f32[28,8,128]{2,1,0:T(8,128)S(1)} %collective-permute-done.10.from_below), custom_call_target="tpu_custom_call" | custom-call | tf_op jit(solution)/shard_map/outer/pallas_call | solution.py:526
  (6 shorter events, 0.0 us)
Async XLA Ops:
  0.0 16.6 %copy-start = (s32[3]{0:T(128)S(1)}, s32[3]{0:T(128)}, u32[]{:S(2)}) copy-start(s32[3]{0:T(128)} %row_shift.1) | copy-start | bytes 40
  0.0 9.3 %collective-permute-start.3 = (f32[8,3,8,128]{3,2,1,0:T(8,128)}, f32[8,3,8,128]{3,2,1,0:T(8,128)S(1)}, u32[]{:S(2)}, u32[]{:S(2)}) collective-permute-start(f32[8,3,8,128]{3,2,1,0:T(8,128)} %param.3), channel_id=1, source_target_pairs={{0,2},{1,3},{2,4},{3,5},{4,6},{5,7},{6,0},{7,1},{8,10},{9,11},{10,... | collective-permute-start | bytes 294920 | tf_op jit(solution)/shard_map/ppermute | solution.py:554
  3.0 9.4 %collective-permute-start = (f32[8,3,8,128]{3,2,1,0:T(8,128)}, f32[8,3,8,128]{3,2,1,0:T(8,128)S(1)}, u32[]{:S(2)}, u32[]{:S(2)}) collective-permute-start(f32[8,3,8,128]{3,2,1,0:T(8,128)} %param.3), channel_id=1, source_target_pairs={{0,4},{1,5},{2,6},{3,7},{4,0},{5,1},{6,2},{7,3},{8,12},{9,13},{10,... | collective-permute-start | bytes 294920 | tf_op jit(solution)/shard_map/ppermute | solution.py:554
  5.6 6.8 %collective-permute-start.5 = (f32[8,3,8,128]{3,2,1,0:T(8,128)}, f32[8,3,8,128]{3,2,1,0:T(8,128)S(1)}, u32[]{:S(2)}, u32[]{:S(2)}) collective-permute-start(f32[8,3,8,128]{3,2,1,0:T(8,128)} %param.3), channel_id=1, source_target_pairs={{0,6},{1,7},{2,0},{3,1},{4,2},{5,3},{6,4},{7,5},{8,14},{9,15},{10,... | collective-permute-start | bytes 294920 | tf_op jit(solution)/shard_map/ppermute | solution.py:554
  7.0 3.7 %collective-permute-start.1 = (s32[3]{0:T(128)}, s32[3]{0:T(128)S(1)}, u32[]{:S(2)}, u32[]{:S(2)}) collective-permute-start(s32[3]{0:T(128)} %row_shift.1), channel_id=1, source_target_pairs={{0,8},{1,25},{2,10},{3,27},{4,12},{5,29},{6,14},{7,31},{8,0},{9,17... | collective-permute-start | bytes 44 | tf_op jit(solution)/shard_map/ppermute | solution.py:550
  9.3 3.1 %collective-permute-start.4 = (f32[8,3,8,128]{3,2,1,0:T(8,128)S(1)}, f32[8,3,8,128]{3,2,1,0:T(8,128)S(1)}, u32[]{:S(2)}, u32[]{:S(2)}) collective-permute-start(f32[8,3,8,128]{3,2,1,0:T(8,128)S(1)} %collective-permute-done.3.refs_1_), channel_id=1, source_target_pairs={{0,1},{1,0},{2,3},{3,2},{4,5},{5,4},{6,7},{7,6},{8,9},{9,8},{10,11... | collective-permute-start | bytes 294920 | tf_op jit(solution)/shard_map/ppermute | solution.py:542
  10.6 1.1 %collective-permute-start.2 = (s32[3]{0:T(128)S(1)}, s32[3]{0:T(128)S(1)}, u32[]{:S(2)}, u32[]{:S(2)}) collective-permute-start(s32[3]{0:T(128)S(1)} %collective-permute-done.1.received), channel_id=1, source_target_pairs={{0,1},{1,0},{2,3},{3,2},{4,5},{5,4},{6,7},{7,6},{8,9},{9,8},{10,11... | collective-permute-start | bytes 44 | tf_op jit(solution)/shard_map/ppermute | solution.py:542
  10.6 2.9 %collective-permute-start.6 = (f32[8,3,8,128]{3,2,1,0:T(8,128)}, f32[8,3,8,128]{3,2,1,0:T(8,128)S(1)}, u32[]{:S(2)}, u32[]{:S(2)}) collective-permute-start(f32[8,3,8,128]{3,2,1,0:T(8,128)} %param.3), channel_id=1, source_target_pairs={{0,1},{1,0},{2,3},{3,2},{4,5},{5,4},{6,7},{7,6},{8,9},{9,8},{10,11... | collective-permute-start | bytes 294920 | tf_op jit(solution)/shard_map/ppermute | solution.py:542
  12.4 1.3 %collective-permute-start.7 = (f32[8,3,8,128]{3,2,1,0:T(8,128)S(1)}, f32[8,3,8,128]{3,2,1,0:T(8,128)S(1)}, u32[]{:S(2)}, u32[]{:S(2)}) collective-permute-start(f32[8,3,8,128]{3,2,1,0:T(8,128)S(1)} %collective-permute-done.refs_2_), channel_id=1, source_target_pairs={{0,1},{1,0},{2,3},{3,2},{4,5},{5,4},{6,7},{7,6},{8,9},{9,8},{10,11... | collective-permute-start | bytes 294920 | tf_op jit(solution)/shard_map/ppermute | solution.py:542
  12.5 1.4 %collective-permute-start.8 = (f32[8,3,8,128]{3,2,1,0:T(8,128)S(1)}, f32[8,3,8,128]{3,2,1,0:T(8,128)S(1)}, u32[]{:S(2)}, u32[]{:S(2)}) collective-permute-start(f32[8,3,8,128]{3,2,1,0:T(8,128)S(1)} %collective-permute-done.5.refs_3_), channel_id=1, source_target_pairs={{0,1},{1,0},{2,3},{3,2},{4,5},{5,4},{6,7},{7,6},{8,9},{9,8},{10,11... | collective-permute-start | bytes 294920 | tf_op jit(solution)/shard_map/ppermute | solution.py:542
  14.1 6.3 %collective-permute-start.9 = (f32[31,8,128]{2,1,0:T(8,128)S(1)}, f32[31,8,128]{2,1,0:T(8,128)S(1)}, u32[]{:S(2)}, u32[]{:S(2)}) collective-permute-start(f32[31,8,128]{2,1,0:T(8,128)S(1)} %get-tuple-element.23), channel_id=1, source_target_pairs={{8,0},{16,8},{24,16},{0,24},{9,1},{17,9},{25,17},{1,25},{10,2},{18... | collective-permute-start | bytes 380936 | tf_op jit(solution)/shard_map/ppermute | solution.py:567
  16.6 6.6 %collective-permute-start.10 = (f32[28,8,128]{2,1,0:T(8,128)S(1)}, f32[28,8,128]{2,1,0:T(8,128)S(1)}, u32[]{:S(2)}, u32[]{:S(2)}) collective-permute-start(f32[28,8,128]{2,1,0:T(8,128)S(1)} %get-tuple-element.24), channel_id=1, source_target_pairs={{0,8},{8,16},{16,24},{24,0},{1,9},{9,17},{17,25},{25,1},{2,10},{10... | collective-permute-start | bytes 344072 | tf_op jit(solution)/shard_map/ppermute | solution.py:566
